TPU v7x, 32 devices: a whole 2x2x4 slice. The times are simulated.
32 devices in a mesh: groups: 2 (over y), tiles: 4 (over z), rows: 2 (over x), comp: 2 (over core).
Axes of the slice: x: 2, y: 2, z: 4, core: 2. Of those that a mesh axis runs over, the one named last changes fastest.
Arguments:
- atmos_grid_state: bfloat16 [256, 256, 256], P(('groups', 'comp'), 'tiles', 'rows'), parts along dimension 0, may hold values from -6 to 6
- sea_field_values: bfloat16 [192, 256, 256], P(('groups', 'comp'), 'tiles', 'rows'), parts along dimension 0, may hold values from -6 to 6
- atmos_depthwise_kernel: float32 [128, 3, 3], P('comp'), may hold values from -2 to 2
- air_from_sea_linear_map: bfloat16 [128, 96], replicated, may hold values from -0.625 to 0.625
- air_standardize_scaling_factor: float32 [128], replicated, may hold values from 0.1 to 1.9
- air_standardize_additive_shift: float32 [128], replicated, may hold values from -3 to 3
- air_widening_linear_map: bfloat16 [256, 128], replicated, may hold values from -0.5 to 0.5
- air_widening_additive_shift: float32 [256], replicated, may hold values from -3 to 3
- air_narrowing_linear_map: bfloat16 [128, 256], replicated, may hold values from -0.375 to 0.375
- ocean_depthwise_kernel: float32 [96, 3, 3], P('comp'), may hold values from -2 to 2
- ocean_coupling_matrix: bfloat16 [96, 128], replicated, may hold values from -0.5 to 0.5
- ocean_layer_norm_gain: float32 [96], replicated, may hold values from 0.1 to 1.9
- ocean_layer_norm_bias: float32 [96], replicated, may hold values from -3 to 3
- ocean_expand_matrix: bfloat16 [192, 96], replicated, may hold values from -0.625 to 0.625
- ocean_expand_offset_bias: float32 [192], replicated, may hold values from -3 to 3
- ocean_project_matrix: bfloat16 [96, 192], replicated, may hold values from -0.4375 to 0.4375
- heat_flux_source_cell: int32 [512, 128], P(('tiles', 'rows')), may hold values from 0 to 8191
- heat_flux_target_cell: int32 [512, 128], P(('tiles', 'rows')), may hold values from 0 to 8191
- heat_flux_margin_weight: float32 [512, 128], P(('tiles', 'rows')), may hold values from 0.25 to 1
- heat_flux_heading: int32 [512, 1], P(('tiles', 'rows')), may hold values from 0 to 8, as said below
- seawarmth_sender_location: int32 [512, 128], P(('tiles', 'rows')), may hold values from 0 to 8191
- seawarmth_receiver_location: int32 [512, 128], P(('tiles', 'rows')), may hold values from 0 to 8191
- seawarmth_overlay_fraction: float32 [512, 128], P(('tiles', 'rows')), may hold values from 0.25 to 1
- seawarmth_direction: int32 [512, 1], P(('tiles', 'rows')), may hold values from 0 to 8, as said below
Outputs:
- atm_next: bfloat16 [256, 256, 256], P(('groups', 'comp'), 'tiles', 'rows'), parts along dimension 0
- ocn_next: bfloat16 [192, 256, 256], P(('groups', 'comp'), 'tiles', 'rows'), parts along dimension 0
There are 2 independent parts, one for each index of `groups`. A program takes and returns all parts, laid end to end along the dimension named above; an argument that names none is the same for every part. Nothing has to cross between parts.
Inputs may be any that keep to these rules, and one draw needn't show every extreme that they name: `heat_flux_heading`: tiles of the first band use no heading below 3; tiles of the last band use neither 6 nor 8. Exactly 16 blocks of every source tile have heading 4, and no heading has more than 16 blocks of one source tile. `seawarmth_direction`: tiles of the first band use no heading below 3; tiles of the last band use neither 6 nor 8. Exactly 16 blocks of every source tile have heading 4, and no heading has more than 16 blocks of one source tile.
All inputs are finite; a program needn't handle non-finite values.
Results may differ from a plain program's by a relative error of at most 0.0058.
Values may be sent and summed in bfloat16 or wider, within the bound.
A program may use at most 128 MiB of HBM per device.

v0:
```python
import jax
import jax.numpy as jnp
from jax import lax
from jax.sharding import PartitionSpec as P


def padded_2(cells, sides, width):
    for axis, dim in sides:
        count = lax.axis_size(axis)
        head = lax.slice_in_dim(cells, 0, width, axis=dim)
        tail = lax.slice_in_dim(cells, cells.shape[dim] - width, cells.shape[dim], axis=dim)
        cells = jnp.concatenate(
            [
                lax.ppermute(tail, axis, [(i, (i + 1) % count) for i in range(count)]),
                cells,
                lax.ppermute(head, axis, [((i + 1) % count, i) for i in range(count)]),
            ],
            axis=dim,
        )
    return cells


def from_partner(block, axis, stride):
    count = lax.axis_size(axis)
    route = []
    for low in range(count):
        high = low | 1 << stride
        if high != low and high < count:
            route += [(low, high), (high, low)]
    return lax.ppermute(block, axis, route)


def packed_margin_rows(field, sources, weights, targets, heading, per_lane):
    chans = field.shape[0]
    flat = field.reshape(chans, -1)
    picked = jnp.take(flat, sources, axis=1)
    values = (picked.astype(jnp.float32) * weights[None]).astype(jnp.bfloat16)
    values = jnp.transpose(values, (1, 0, 2))
    lanes = heading[:, 0]
    match = lanes[:, None] == jnp.arange(9, dtype=jnp.int32)[None, :]
    counts = jnp.cumsum(match.astype(jnp.int32), axis=0) - 1
    within = jnp.sum(jnp.where(match, counts, 0), axis=1)
    slots = lanes * per_lane + within
    width = sources.shape[1]
    outgoing = jnp.zeros((9 * per_lane, chans, width), jnp.bfloat16).at[slots].set(values)
    where_to = jnp.zeros((9 * per_lane, width), jnp.int32).at[slots].set(targets)
    return (
        outgoing.reshape((3, 3, per_lane, chans, width)),
        where_to.reshape((3, 3, per_lane, width)),
    )


def arrived_entries(received, where_to, height, width):
    chans = received.shape[1]
    spread = jnp.transpose(received, (1, 0, 2)).reshape(chans, -1).astype(jnp.float32)
    total = jnp.zeros((chans, height * width), jnp.float32).at[:, where_to.reshape(-1)].add(spread)
    return total.astype(jnp.bfloat16).reshape(chans, height, width)


def send_margin_rows(
    heat_flux_outbound, heat_flux_placement, surface_temp_outbound, surface_temp_placement
):
    band = lax.axis_index("tiles")
    last_band = lax.axis_size("tiles") - 1
    pieces = []
    wide = (
        padded_2(heat_flux_outbound, (("tiles", 0), ("rows", 1)), 1),
        padded_2(heat_flux_placement, (("tiles", 0), ("rows", 1)), 1),
        padded_2(surface_temp_outbound, (("tiles", 0), ("rows", 1)), 1),
        padded_2(surface_temp_placement, (("tiles", 0), ("rows", 1)), 1),
    )
    for lift in (-1, 0, 1):
        for sideways in (-1, 0, 1):
            got = tuple((member[2 - 2 * lift, 2 - 2 * sideways] for member in wide))
            if lift == 1:
                usable = band != 0
                got = (jnp.where(usable, got[0], 0), got[1], jnp.where(usable, got[2], 0), got[3])
            elif lift == -1:
                usable = band != last_band
                got = (jnp.where(usable, got[0], 0), got[1], jnp.where(usable, got[2], 0), got[3])
            pieces.append(got)
    folded_blocks = (
        heat_flux_outbound[2, 1],
        heat_flux_placement[2, 1],
        surface_temp_outbound[2, 1],
        surface_temp_placement[2, 1],
    )
    for bit in range(lax.axis_size("rows").bit_length() - 1):
        folded_blocks = from_partner(
            (folded_blocks[0], folded_blocks[1], folded_blocks[2], folded_blocks[3]), "rows", bit
        )
    at_fold = band == last_band
    pieces.append(
        (
            jnp.where(at_fold, folded_blocks[0], 0),
            folded_blocks[1],
            jnp.where(at_fold, folded_blocks[2], 0),
            folded_blocks[3],
        )
    )
    return tuple((jnp.concatenate([piece[item] for piece in pieces], axis=0) for item in range(4)))


def extend(field, folded_blocks):
    padded = padded_2(field, (("tiles", 1), ("rows", 2)), 1)
    band = lax.axis_index("tiles")
    last_band = lax.axis_size("tiles") - 1
    height = field.shape[1]
    zero_row = jnp.zeros_like(padded[:, 0, :])
    south = jnp.where(band == 0, zero_row, padded[:, 0, :])
    if folded_blocks:
        mirror = padded[:, height, :]
        for bit in range(lax.axis_size("rows").bit_length() - 1):
            mirror = from_partner(mirror, "rows", bit)
        cap = mirror[:, ::-1]
    else:
        cap = zero_row
    north = jnp.where(band == last_band, cap, padded[:, height + 1, :])
    return padded.at[:, 0, :].set(south).at[:, height + 1, :].set(north)


def depthwise(field, kernel, folded_blocks):
    padded = extend(field, folded_blocks)
    height, width = (field.shape[1], field.shape[2])
    total = jnp.zeros(field.shape, jnp.float32)
    for row in range(3):
        for col in range(3):
            total = total + kernel[:, row, col][:, None, None] * padded[
                :, row : row + height, col : col + width
            ].astype(jnp.float32)
    return total.astype(jnp.bfloat16)


def hidden_units(conv, coupled, coupling, gain, shift, expand, expand_bias):
    mixed = conv.astype(jnp.float32) + jnp.einsum(
        "cq,qyx->cyx", coupling, coupled, preferred_element_type=jnp.float32
    )
    mean = jnp.mean(mixed, axis=0, keepdims=True)
    centred = mixed - mean
    var = jnp.mean(centred * centred, axis=0, keepdims=True)
    normed = (centred * lax.rsqrt(var + 1e-06) * gain[:, None, None] + shift[:, None, None]).astype(
        jnp.bfloat16
    )
    hidden = (
        jnp.einsum("hc,cyx->hyx", expand, normed, preferred_element_type=jnp.float32)
        + expand_bias[:, None, None]
    )
    return jax.nn.gelu(hidden, approximate=True).astype(jnp.bfloat16)


def block(
    state, coupled, kernel, coupling, gain, shift, expand, expand_bias, project, folded_blocks
):
    conv = depthwise(state, kernel, folded_blocks)
    hidden = hidden_units(
        lax.all_to_all(conv, "comp", split_axis=1, concat_axis=0, tiled=True),
        lax.all_to_all(coupled, "comp", split_axis=1, concat_axis=0, tiled=True),
        coupling,
        gain,
        shift,
        expand,
        expand_bias,
    )
    whole = jnp.einsum("ch,hyx->cyx", project, hidden, preferred_element_type=jnp.float32).astype(
        jnp.bfloat16
    )
    update = lax.all_to_all(whole, "comp", split_axis=0, concat_axis=1, tiled=True)
    return (state.astype(jnp.float32) + update.astype(jnp.float32)).astype(jnp.bfloat16)


def local(
    atmos_grid_state,
    sea_field_values,
    atmos_depthwise_kernel,
    air_from_sea_linear_map,
    air_standardize_scaling_factor,
    air_standardize_additive_shift,
    air_widening_linear_map,
    air_widening_additive_shift,
    air_narrowing_linear_map,
    ocean_depthwise_kernel,
    ocean_coupling_matrix,
    ocean_layer_norm_gain,
    ocean_layer_norm_bias,
    ocean_expand_matrix,
    ocean_expand_offset_bias,
    ocean_project_matrix,
    heat_flux_source_cell,
    heat_flux_target_cell,
    heat_flux_margin_weight,
    heat_flux_heading,
    seawarmth_sender_location,
    seawarmth_receiver_location,
    seawarmth_overlay_fraction,
    seawarmth_direction,
):
    flux_lane = heat_flux_heading.shape[0] // 4
    surface_temp_column = seawarmth_direction.shape[0] // 4
    heat_flux_outbound, heat_flux_placement = packed_margin_rows(
        atmos_grid_state,
        heat_flux_source_cell,
        heat_flux_margin_weight,
        heat_flux_target_cell,
        heat_flux_heading,
        flux_lane,
    )
    surface_temp_outbound, surface_temp_placement = packed_margin_rows(
        sea_field_values,
        seawarmth_sender_location,
        seawarmth_overlay_fraction,
        seawarmth_receiver_location,
        seawarmth_direction,
        surface_temp_column,
    )
    heat_flux_incoming, heat_flux_gathered, surface_temp_incoming, surface_temp_gathered = (
        send_margin_rows(
            heat_flux_outbound, heat_flux_placement, surface_temp_outbound, surface_temp_placement
        )
    )
    flux = arrived_entries(
        heat_flux_incoming, heat_flux_gathered, sea_field_values.shape[1], sea_field_values.shape[2]
    )
    seawater_warmth = arrived_entries(
        surface_temp_incoming,
        surface_temp_gathered,
        atmos_grid_state.shape[1],
        atmos_grid_state.shape[2],
    )
    atm_next = block(
        atmos_grid_state,
        seawater_warmth,
        atmos_depthwise_kernel,
        air_from_sea_linear_map,
        air_standardize_scaling_factor,
        air_standardize_additive_shift,
        air_widening_linear_map,
        air_widening_additive_shift,
        air_narrowing_linear_map,
        False,
    )
    ocn_next = block(
        sea_field_values,
        flux,
        ocean_depthwise_kernel,
        ocean_coupling_matrix,
        ocean_layer_norm_gain,
        ocean_layer_norm_bias,
        ocean_expand_matrix,
        ocean_expand_offset_bias,
        ocean_project_matrix,
        True,
    )
    return (atm_next, ocn_next)


def solution(mesh):
    placed = (
        P(("groups", "comp"), "tiles", "rows"),
        P(("groups", "comp"), "tiles", "rows"),
        P("comp", None, None),
        P(),
        P(),
        P(),
        P(),
        P(),
        P(),
        P("comp", None, None),
        P(),
        P(),
        P(),
        P(),
        P(),
        P(),
        P(("tiles", "rows"), None),
        P(("tiles", "rows"), None),
        P(("tiles", "rows"), None),
        P(("tiles", "rows"), None),
        P(("tiles", "rows"), None),
        P(("tiles", "rows"), None),
        P(("tiles", "rows"), None),
        P(("tiles", "rows"), None),
    )
    return jax.shard_map(
        local,
        mesh=mesh,
        in_specs=placed,
        out_specs=(P(("groups", "comp"), "tiles", "rows"), P(("groups", "comp"), "tiles", "rows")),
        check_vma=False,
    )
```

profile of v0, /device:TPU:29, one launch (start us, length us, event | category | flops | bytes accessed | tf_op | source)
XLA Modules:
  0.0 604.7 jit_solution(10508579274967777900)
XLA Ops:
  8.6 29.2 %gather_fusion.1 = bf16[8192,64]{1,0:T(8,128)(2,1)} fusion(bf16[64,8192]{0,1:T(8,128)(2,1)S(1)} %bitcast.343, s32[8192]{0:T(1024)S(1)} %get-tuple-element.102), kind=kCustom, calls=%fused_computation.1 | custom fusion | bytes 2129920 | tf_op jit(solution)/shard_map/jit(_take)/gather | solution.py:36
  61.2 29.2 %gather_fusion = bf16[8192,48]{1,0:T(8,128)(2,1)} fusion(bf16[48,8192]{0,1:T(8,128)(2,1)S(1)} %bitcast.344, s32[8192]{0:T(1024)S(1)} %copy-done.22), kind=kCustom, calls=%fused_computation | custom fusion | bytes 1605632 | tf_op jit(solution)/shard_map/jit(_take)/gather | solution.py:36
  93.9 6.1 %scatter_fusion = bf16[144,48,128]{2,1,0:T(8,128)(2,1)S(1)} fusion(bf16[144,48,128]{2,1,0:T(8,128)(2,1)S(1)} %broadcast_in_dim.94, s32[64]{0:T(128)S(1)} %copy-done.53, bf16[64,48,128]{2,1,0:T(8,128)(2,1)} %fusion.37), kind=kCustom, calls=%fused_computation.3 | custom fusion | bytes 2359552 | tf_op jit(solution)/shard_map/scatter | solution.py:45
  129.5 3.3 collective-permute-start.4
  142.8 3.7 pad_maximum_fusion
  150.5 5.3 add_convert_fusion.1
  156.6 10.5 %all_to_all.72 = bf16[64,64,128]{2,0,1:T(8,128)(2,1)S(1)} all-to-all(bf16[64,64,128]{2,0,1:T(8,128)(2,1)S(1)} %copy.146), channel_id=1, replica_groups=mesh['groups'=2,'tiles'=4,'rows'=2,'comp'=2] {'comp'}, dimensions={1} | all-to-all | bytes 2097152 | tf_op jit(solution)/shard_map/all_to_all | solution.py:156
  171.5 6.5 %add_convert_fusion.3 = bf16[48,64,128]{2,0,1:T(8,128)(2,1)S(1)} fusion(bf16[48,66,130]{2,0,1:T(8,128)(2,1)} %fusion.90, f32[48]{0:T(128)S(1)} %copy-done.51, f32[48]{0:T(128)S(1)} %copy-done.52, f32[48]{0:T(128)S(1)} %copy-done.45, f32[48]{0:T(128)S(1)} %copy-done.46, f32[48]{0:T(128)S(1)} %copy-done.47, f32[48]{0:T(128)S(1)} %copy-done.48, ...), kind=kLoop, calls=%fused_computation.50 | loop fusion | flops 10616832 | bytes 7866048 | tf_op jit(solution)/shard_map/convert_element_type | solution.py:131
  178.1 4.8 all_to_all.73
  187.1 3.7 collective-permute-start.9
  206.0 3.0 pad_maximum_fusion.2
  209.9 15.7 %collective-permute-done.11 = bf16[5,1,16,48,128]{4,3,2,1,0:T(8,128)(2,1)S(1)} collective-permute-done((bf16[5,1,16,48,128]{4,3,2,1,0:T(8,128)(2,1)S(1)}, bf16[5,1,16,48,128]{4,3,2,1,0:T(8,128)(2,1)S(1)}, u32[]{:S(2)}, u32[]{:S(2)}) %collective-permute-start.11) | collective-permute-done | bytes 983072 | tf_op jit(solution)/shard_map/ppermute | solution.py:16
  226.9 19.8 %collective-permute-done.12 = bf16[5,1,16,48,128]{4,3,2,1,0:T(8,128)(2,1)S(1)} collective-permute-done((bf16[5,1,16,48,128]{4,3,2,1,0:T(8,128)(2,1)S(1)}, bf16[5,1,16,48,128]{4,3,2,1,0:T(8,128)(2,1)S(1)}, u32[]{:S(2)}, u32[]{:S(2)}) %collective-permute-start.12) | collective-permute-done | bytes 983072 | tf_op jit(solution)/shard_map/ppermute | solution.py:14
  247.0 3.9 collective-permute-done.13
  253.2 7.7 %copy.150 = f32[48,160,128]{0,2,1:T(8,128)} copy(f32[48,160,128]{2,0,1:T(8,128)} %convert_bitcast_fusion.1) | data formatting | bytes 7864320 | tf_op jit(solution)/shard_map/convert_element_type | solution.py:55
  260.9 132.2 %scatter_custom_fusion.2 = f32[48,8192]{0,1:T(8,128)} fusion(s32[20480]{0:T(1024)} %bitcast.375, f32[20480,48]{1,0:T(8,128)} %bitcast.351, f32[]{:T(128)} %constant.164.clone.1), kind=kCustom, calls=%fused_computation.38 | custom fusion | flops 983040 | bytes 1573376 | tf_op jit(solution)/shard_map/scatter-add | solution.py:56
  393.0 3.7 convert_element_type.236
  399.4 15.4 %all_to_all.74 = bf16[48,64,128]{2,0,1:T(8,128)(2,1)S(1)} all-to-all(bf16[48,64,128]{2,0,1:T(8,128)(2,1)} %copy.151), channel_id=1, replica_groups=mesh['groups'=2,'tiles'=4,'rows'=2,'comp'=2] {'comp'}, dimensions={1} | all-to-all | bytes 1572864 | tf_op jit(solution)/shard_map/all_to_all | solution.py:157
  417.7 4.6 fusion.26
  424.9 5.9 all_to_all.75
  445.0 8.4 %copy.167 = f32[64,160,128]{0,2,1:T(8,128)} copy(f32[64,160,128]{2,0,1:T(8,128)} %convert_bitcast_fusion) | data formatting | bytes 10485760 | tf_op jit(solution)/shard_map/convert_element_type | solution.py:55
  453.4 132.2 %scatter_custom_fusion.5 = f32[64,8192]{0,1:T(8,128)} fusion(s32[20480]{0:T(1024)S(1)} %bitcast.374, f32[20480,64]{1,0:T(8,128)} %bitcast.352, f32[]{:T(128)} %constant.164.clone.1), kind=kCustom, calls=%fused_computation.34 | custom fusion | flops 1310720 | bytes 2097664 | tf_op jit(solution)/shard_map/scatter-add | solution.py:56
  588.9 4.7 all_to_all.76
  597.4 4.4 all_to_all.77
  (302 shorter events, 138.6 us)
Async XLA Ops:
  47.2 158.2 %collective-permute-start.24 = (bf16[1,3,16,64,128]{4,3,2,1,0:T(8,128)(2,1)}, bf16[1,3,16,64,128]{4,3,2,1,0:T(8,128)(2,1)}, u32[]{:S(2)}, u32[]{:S(2)}) collective-permute-start(bf16[1,3,16,64,128]{4,3,2,1,0:T(8,128)(2,1)} %bitcast.101), channel_id=1, source_target_pairs={{0,4},{4,8},{8,12},{12,0},{1,5},{5,9},{9,13},{13,1},{2,6},{6,10},{... | collective-permute-start | bytes 2359304 | tf_op jit(solution)/shard_map/ppermute | solution.py:14
  47.2 158.8 %collective-permute-start.25 = (bf16[1,3,16,64,128]{4,3,2,1,0:T(8,128)(2,1)}, bf16[1,3,16,64,128]{4,3,2,1,0:T(8,128)(2,1)}, u32[]{:S(2)}, u32[]{:S(2)}) collective-permute-start(bf16[1,3,16,64,128]{4,3,2,1,0:T(8,128)(2,1)} %bitcast.103), channel_id=1, source_target_pairs={{4,0},{8,4},{12,8},{0,12},{5,1},{9,5},{13,9},{1,13},{6,2},{10,6},{... | collective-permute-start | bytes 2359304 | tf_op jit(solution)/shard_map/ppermute | solution.py:16
  50.3 79.2 %collective-permute-start.19 = (s32[1,3,16,128]{3,2,1,0:T(8,128)}, s32[1,3,16,128]{3,2,1,0:T(8,128)}, u32[]{:S(2)}, u32[]{:S(2)}) collective-permute-start(s32[1,3,16,128]{3,2,1,0:T(8,128)} %bitcast.82), channel_id=1, source_target_pairs={{0,4},{4,8},{8,12},{12,0},{1,5},{5,9},{9,13},{13,1},{2,6},{6,10},{... | collective-permute-start | bytes 73736 | tf_op jit(solution)/shard_map/ppermute | solution.py:14
  53.7 51.1 %collective-permute-start.14 = (bf16[48,1,128]{2,0,1:T(8,128)(2,1)}, bf16[48,1,128]{2,0,1:T(8,128)(2,1)}, u32[]{:S(2)}, u32[]{:S(2)}) collective-permute-start(bf16[48,1,128]{2,0,1:T(8,128)(2,1)} %copy.179), channel_id=1, source_target_pairs={{0,4},{4,8},{8,12},{12,0},{1,5},{5,9},{9,13},{13,1},{2,6},{6,10},{... | collective-permute-start | bytes 36872 | tf_op jit(solution)/shard_map/ppermute | solution.py:14
  54.3 54.7 %collective-permute-start.15 = (bf16[48,1,128]{2,0,1:T(8,128)(2,1)}, bf16[48,1,128]{2,0,1:T(8,128)(2,1)}, u32[]{:S(2)}, u32[]{:S(2)}) collective-permute-start(bf16[48,1,128]{2,0,1:T(8,128)(2,1)} %copy.180), channel_id=1, source_target_pairs={{4,0},{8,4},{12,8},{0,12},{5,1},{9,5},{13,9},{1,13},{6,2},{10,6},{... | collective-permute-start | bytes 36872 | tf_op jit(solution)/shard_map/ppermute | solution.py:16
  104.8 7.8 %collective-permute-start = (bf16[64,1,128]{2,0,1:T(8,128)(2,1)S(1)}, bf16[64,1,128]{2,0,1:T(8,128)(2,1)S(1)}, u32[]{:S(2)}, u32[]{:S(2)}) collective-permute-start(bf16[64,1,128]{2,0,1:T(8,128)(2,1)S(1)} %copy.176), channel_id=1, source_target_pairs={{0,4},{4,8},{8,12},{12,0},{1,5},{5,9},{9,13},{13,1},{2,6},{6,10},{... | collective-permute-start | bytes 49160 | tf_op jit(solution)/shard_map/ppermute | solution.py:14
  109.0 4.8 collective-permute-start.1
  112.5 8.5 %collective-permute-start.16 = (bf16[48,66,1]{1,0,2:T(8,128)(2,1)S(1)}, bf16[48,66,1]{1,0,2:T(8,128)(2,1)S(1)}, u32[]{:S(2)}, u32[]{:S(2)}) collective-permute-start(bf16[48,66,1]{1,0,2:T(8,128)(2,1)S(1)} %copy.160), channel_id=1, source_target_pairs={{0,2},{2,0},{1,3},{3,1},{4,6},{6,4},{5,7},{7,5},{8,10},{10,8},{9,1... | collective-permute-start | bytes 19016 | tf_op jit(solution)/shard_map/ppermute | solution.py:14
  113.9 8.1 %collective-permute-start.17 = (bf16[48,66,1]{1,0,2:T(8,128)(2,1)S(1)}, bf16[48,66,1]{1,0,2:T(8,128)(2,1)S(1)}, u32[]{:S(2)}, u32[]{:S(2)}) collective-permute-start(bf16[48,66,1]{1,0,2:T(8,128)(2,1)S(1)} %copy.161), channel_id=1, source_target_pairs={{2,0},{0,2},{3,1},{1,3},{6,4},{4,6},{7,5},{5,7},{10,8},{8,10},{11,... | collective-permute-start | bytes 19016 | tf_op jit(solution)/shard_map/ppermute | solution.py:16
  121.0 11.7 %collective-permute-start.20 = (s32[1,3,16,128]{3,2,1,0:T(8,128)}, s32[1,3,16,128]{3,2,1,0:T(8,128)}, u32[]{:S(2)}, u32[]{:S(2)}) collective-permute-start(s32[1,3,16,128]{3,2,1,0:T(8,128)} %bitcast.84), channel_id=1, source_target_pairs={{4,0},{8,4},{12,8},{0,12},{5,1},{9,5},{13,9},{1,13},{6,2},{10,6},{... | collective-permute-start | bytes 73736 | tf_op jit(solution)/shard_map/ppermute | solution.py:16
  122.5 69.0 %collective-permute-start.23 = (s32[16,128]{1,0:T(8,128)S(1)}, s32[16,128]{1,0:T(8,128)}, u32[]{:S(2)}, u32[]{:S(2)}) collective-permute-start(s32[16,128]{1,0:T(8,128)S(1)} %slice_bitcast_fusion.10), channel_id=1, source_target_pairs={{0,2},{2,0},{1,3},{3,1},{4,6},{6,4},{5,7},{7,5},{8,10},{10,8},{9,1... | collective-permute-start | bytes 24584 | tf_op jit(solution)/shard_map/ppermute | solution.py:30
  129.5 4.7 collective-permute-start.4
  132.8 4.5 collective-permute-start.5
  134.2 4.5 collective-permute-start.2
  138.7 62.4 %collective-permute-start.10 = (bf16[1,3,16,48,128]{4,3,2,1,0:T(8,128)(2,1)}, bf16[1,3,16,48,128]{4,3,2,1,0:T(8,128)(2,1)}, u32[]{:S(2)}, u32[]{:S(2)}) collective-permute-start(bf16[1,3,16,48,128]{4,3,2,1,0:T(8,128)(2,1)} %bitcast.36), channel_id=1, source_target_pairs={{4,0},{8,4},{12,8},{0,12},{5,1},{9,5},{13,9},{1,13},{6,2},{10,6},{... | collective-permute-start | bytes 1769480 | tf_op jit(solution)/shard_map/ppermute | solution.py:16
  140.4 28.3 %collective-permute-start.18 = (bf16[48,130]{1,0:T(8,128)(2,1)}, bf16[48,130]{1,0:T(8,128)(2,1)}, u32[]{:S(2)}, u32[]{:S(2)}) collective-permute-start(bf16[48,130]{1,0:T(8,128)(2,1)} %get-tuple-element.60), channel_id=1, source_target_pairs={{0,2},{2,0},{1,3},{3,1},{4,6},{6,4},{5,7},{7,5},{8,10},{10,8},{9,1... | collective-permute-start | bytes 37448 | tf_op jit(solution)/shard_map/ppermute | solution.py:30
  168.7 15.5 %collective-permute-start.21 = (s32[5,1,16,128]{3,2,1,0:T(8,128)S(1)}, s32[5,1,16,128]{3,2,1,0:T(8,128)S(1)}, u32[]{:S(2)}, u32[]{:S(2)}) collective-permute-start(s32[5,1,16,128]{3,2,1,0:T(8,128)S(1)} %copy-done.30), channel_id=1, source_target_pairs={{2,0},{0,2},{3,1},{1,3},{6,4},{4,6},{7,5},{5,7},{10,8},{8,10},{11,... | collective-permute-start | bytes 122888 | tf_op jit(solution)/shard_map/ppermute | solution.py:16
  187.1 14.8 %collective-permute-start.9 = (bf16[1,3,16,48,128]{4,3,2,1,0:T(8,128)(2,1)S(1)}, bf16[1,3,16,48,128]{4,3,2,1,0:T(8,128)(2,1)S(1)}, u32[]{:S(2)}, u32[]{:S(2)}) collective-permute-start(bf16[1,3,16,48,128]{4,3,2,1,0:T(8,128)(2,1)S(1)} %bitcast.371), channel_id=1, source_target_pairs={{0,4},{4,8},{8,12},{12,0},{1,5},{5,9},{9,13},{13,1},{2,6},{6,10},{... | collective-permute-start | bytes 1769480 | tf_op jit(solution)/shard_map/ppermute | solution.py:14
  200.8 240.2 %collective-permute-start.28 = (bf16[16,64,128]{2,1,0:T(8,128)(2,1)}, bf16[16,64,128]{2,1,0:T(8,128)(2,1)}, u32[]{:S(2)}, u32[]{:S(2)}) collective-permute-start(bf16[16,64,128]{2,1,0:T(8,128)(2,1)} %slice_bitcast_fusion), channel_id=1, source_target_pairs={{0,2},{2,0},{1,3},{3,1},{4,6},{6,4},{5,7},{7,5},{8,10},{10,8},{9,1... | collective-permute-start | bytes 786440 | tf_op jit(solution)/shard_map/ppermute | solution.py:30
  203.2 22.4 %collective-permute-start.11 = (bf16[5,1,16,48,128]{4,3,2,1,0:T(8,128)(2,1)S(1)}, bf16[5,1,16,48,128]{4,3,2,1,0:T(8,128)(2,1)S(1)}, u32[]{:S(2)}, u32[]{:S(2)}) collective-permute-start(bf16[5,1,16,48,128]{4,3,2,1,0:T(8,128)(2,1)S(1)} %get-tuple-element.53), channel_id=1, source_target_pairs={{2,0},{0,2},{3,1},{1,3},{6,4},{4,6},{7,5},{5,7},{10,8},{8,10},{11,... | collective-permute-start | bytes 2949128 | tf_op jit(solution)/shard_map/ppermute | solution.py:16
  203.8 42.9 %collective-permute-start.12 = (bf16[5,1,16,48,128]{4,3,2,1,0:T(8,128)(2,1)S(1)}, bf16[5,1,16,48,128]{4,3,2,1,0:T(8,128)(2,1)S(1)}, u32[]{:S(2)}, u32[]{:S(2)}) collective-permute-start(bf16[5,1,16,48,128]{4,3,2,1,0:T(8,128)(2,1)S(1)} %get-tuple-element.52), channel_id=1, source_target_pairs={{0,2},{2,0},{1,3},{3,1},{4,6},{6,4},{5,7},{7,5},{8,10},{10,8},{9,1... | collective-permute-start | bytes 2949128 | tf_op jit(solution)/shard_map/ppermute | solution.py:14
  205.4 45.5 %collective-permute-start.13 = (bf16[16,48,128]{2,1,0:T(8,128)(2,1)S(1)}, bf16[16,48,128]{2,1,0:T(8,128)(2,1)S(1)}, u32[]{:S(2)}, u32[]{:S(2)}) collective-permute-start(bf16[16,48,128]{2,1,0:T(8,128)(2,1)S(1)} %copy-done.21), channel_id=1, source_target_pairs={{0,2},{2,0},{1,3},{3,1},{4,6},{6,4},{5,7},{7,5},{8,10},{10,8},{9,1... | collective-permute-start | bytes 589832 | tf_op jit(solution)/shard_map/ppermute | solution.py:30
  208.9 223.8 %collective-permute-start.26 = (bf16[5,1,16,64,128]{4,3,2,1,0:T(8,128)(2,1)}, bf16[5,1,16,64,128]{4,3,2,1,0:T(8,128)(2,1)}, u32[]{:S(2)}, u32[]{:S(2)}) collective-permute-start(bf16[5,1,16,64,128]{4,3,2,1,0:T(8,128)(2,1)} %get-tuple-element.51), channel_id=1, source_target_pairs={{2,0},{0,2},{3,1},{1,3},{6,4},{4,6},{7,5},{5,7},{10,8},{8,10},{11,... | collective-permute-start | bytes 3932168 | tf_op jit(solution)/shard_map/ppermute | solution.py:16
  225.6 209.2 %collective-permute-start.27 = (bf16[5,1,16,64,128]{4,3,2,1,0:T(8,128)(2,1)}, bf16[5,1,16,64,128]{4,3,2,1,0:T(8,128)(2,1)}, u32[]{:S(2)}, u32[]{:S(2)}) collective-permute-start(bf16[5,1,16,64,128]{4,3,2,1,0:T(8,128)(2,1)} %get-tuple-element.50), channel_id=1, source_target_pairs={{0,2},{2,0},{1,3},{3,1},{4,6},{6,4},{5,7},{7,5},{8,10},{10,8},{9,1... | collective-permute-start | bytes 3932168 | tf_op jit(solution)/shard_map/ppermute | solution.py:14
  (63 other events, 786.2 us)
where the time goes:
time: 615 us; the launch traced here: 605 us
  other arithmetic  325 us (53%)
  local copies, waits for them, and re-layouts  150 us (24%)
  waiting for transfers between devices  49.1 us (8%)
  blocking collectives  45.7 us (7%)
  starting transfers between devices  24.8 us (4%)
  matrix products  8 us (1%)
    scatter-add x2, other arithmetic, arrived_entries(): jnp.zeros((chans, height * width), jnp.float32).at[:, where_to.reshape(-1)]  264 us
    gather x4, local copies, waits for them, and re-layouts, packed_margin_rows(): picked = jnp.take(flat, sources, axis=1)  62.4 us
    ppermute x12, waiting for transfers between devices, padded_2(): lax.ppermute(tail, axis, [(i, (i + 1) % count) for i in range(count)])  23.9 us
    unnamed x150, local copies, waits for them, and re-layouts  22.5 us
    ppermute x12, waiting for transfers between devices, padded_2(): lax.ppermute(head, axis, [((i + 1) % count, i) for i in range(count)])  20.1 us
    all_to_all x2, blocking collectives, block(): lax.all_to_all(coupled, 'comp', split_axis=1, concat_axis=0, tiled=True)  20.1 us
    convert_element_type x2, local copies, waits for them, and re-layouts, arrived_entries(): jnp.transpose(received, (1, 0, 2)).reshape(chans, -1).astype(jnp.float32)  16.1 us
    all_to_all x2, blocking collectives, block(): lax.all_to_all(conv, 'comp', split_axis=1, concat_axis=0, tiled=True)  15.3 us
  transfers between devices with their start and end apart: 29, of which 9 were waited for; matrix products, arithmetic and copies ran while one was open for 46% of the time, Pallas kernels for 0%

commit v1 on v0

v1 whole, which is shorter than its diff:
```python
import functools

import jax
import jax.numpy as jnp
from jax import lax
from jax.experimental import pallas as pl
from jax.experimental.pallas import tpu as pltpu
from jax.sharding import PartitionSpec as P

SLOTS = 16
META = 112
LANES = 256
GROUP = 8
VMEM_LIMIT = 56 * 1024 * 1024
BF = jnp.bfloat16
F32 = jnp.float32
MESH = pl.DeviceIdType.MESH


def pack_kernel(bounds, slots_ref, state_ref, halo_ref, pos_ref, high_ref, weight_ref, meta_ref, out_ref):
    flat_slots = SLOTS + 1
    pairs = state_ref.shape[0] // 2

    def clear(i, _):
        out_ref[i // SLOTS, lax.rem(i, SLOTS), META:, :] = jnp.full((16, 128), -1, BF)
        return 0

    lax.fori_loop(0, 9 * SLOTS, clear, 0)
    for k in range(9):
        out_ref[k, flat_slots - 1] = halo_ref[k]
    column = lax.broadcasted_iota(jnp.int32, (LANES, LANES), 0).astype(F32).astype(BF)
    row16 = lax.broadcasted_iota(jnp.int32, (16, 128), 0)

    def step(j, _):
        for f, (low, high) in enumerate(bounds):
            chans = high - low
            hit = jnp.broadcast_to(pos_ref[f, j], (LANES, LANES)).astype(BF) == column
            onehot = jnp.where(hit, jnp.ones((), BF), jnp.zeros((), BF))
            wanted = jnp.broadcast_to(high_ref[f, j], (chans, LANES))
            total = jnp.zeros((chans, LANES), F32)
            for first in range(0, pairs, GROUP):
                lhs = jnp.concatenate(
                    [
                        jnp.concatenate(
                            [state_ref[2 * q, low:high, :], state_ref[2 * q + 1, low:high, :]], axis=1
                        )
                        for q in range(first, first + GROUP)
                    ],
                    axis=0,
                )
                part = jnp.dot(lhs, onehot, preferred_element_type=F32)
                for q in range(GROUP):
                    total = jnp.where(
                        wanted == float(first + q), part[q * chans : (q + 1) * chans], total
                    )
            values = (total * weight_ref[f, j]).astype(BF)
            for half in range(2):
                block = 2 * j + half
                slot = slots_ref[f, block]
                k, s = slot // SLOTS, lax.rem(slot, SLOTS)
                out_ref[k, s, low:high, :] = values[:, half * 128 : (half + 1) * 128]
                old = out_ref[k, s, META:, :].astype(F32)
                for item in range(2):
                    place = jnp.broadcast_to(meta_ref[f, item, block], (16, 128))
                    old = jnp.where(row16 == 2 * f + item, place, old)
                out_ref[k, s, META:, :] = old.astype(BF)
        return 0

    lax.fori_loop(0, slots_ref.shape[1] // 2, step, 0)


def send_kernel(n_tiles, n_rows, packed_ref, got_ref, send_sem, recv_sem, local_sem):
    band = lax.axis_index("tiles")
    strip = lax.axis_index("rows")
    last = n_tiles - 1
    barrier = pltpu.get_barrier_semaphore()
    routes = []
    for k in (0, 2, 6, 8, 3, 5, 1, 7):
        lift, side = k // 3 - 1, k % 3 - 1
        to = {"tiles": band + lift, "rows": lax.rem(strip + side + n_rows, n_rows)}
        sends = (band + lift >= 0) & (band + lift <= last)
        receives = (band - lift >= 0) & (band - lift <= last)
        routes.append((k, k, to, sends, receives))
    routes.append((7, 9, {"rows": n_rows - 1 - strip}, band == last, band == last))

    peers = []
    for lift in (-1, 0, 1):
        for side in (0, 1) if n_rows == 2 else (-1, 0, 1):
            if (lift, side) != (0, 0):
                to = {"tiles": band + lift, "rows": lax.rem(strip + side + n_rows, n_rows)}
                peers.append((to, (band + lift >= 0) & (band + lift <= last)))
    if n_rows > 2:
        mirror = n_rows - 1 - strip
        beside = (mirror == lax.rem(strip + 1, n_rows)) | (mirror == lax.rem(strip + n_rows - 1, n_rows))
        peers.append(({"rows": mirror}, (band == last) & jnp.logical_not(beside)))
    for to, there in peers:

        @pl.when(there)
        def _():
            pl.semaphore_signal(barrier, inc=1, device_id=to, device_id_type=MESH)

    pl.semaphore_wait(barrier, sum(there.astype(jnp.int32) for _, there in peers))

    def copy(i):
        src, dst, to, _, _ = routes[i]
        return pltpu.make_async_remote_copy(
            src_ref=packed_ref.at[src],
            dst_ref=got_ref.at[dst],
            send_sem=send_sem.at[i],
            recv_sem=recv_sem.at[i],
            device_id=to,
            device_id_type=MESH,
        )

    for i, route in enumerate(routes):

        @pl.when(route[3])
        def _():
            copy(i).start()

    own = pltpu.make_async_copy(packed_ref.at[4], got_ref.at[4], local_sem)
    own.start()
    own.wait()
    for i, route in enumerate(routes):

        @pl.when(route[3])
        def _():
            copy(i).wait_send()

        @pl.when(route[4])
        def _():
            copy(i).wait_recv()


def land_kernel(
    bounds, outs, order_ref, count_ref, got_ref, state_ref, edge_ref, cols_ref, taps_ref,
    out_ref, acc_ref,
):
    height = state_ref.shape[0]
    chans = state_ref.shape[1]
    row_of = lax.broadcasted_iota(jnp.int32, (256, 128), 0)
    lane_of = lax.broadcasted_iota(jnp.int32, (256, 128), 1)
    lane = lax.broadcasted_iota(jnp.int32, (chans, 128), 1)
    cols = cols_ref[...]

    def taps(i, row):
        pick = ((row_of == i) & (lane_of == 0)) | ((row_of == i + 128) & (lane_of == 127))
        ends = jnp.dot(cols, pick.astype(F32).astype(BF), preferred_element_type=F32)
        row = row.astype(F32)
        left = jnp.where(lane == 0, ends, pltpu.roll(row, 1, 1))
        right = jnp.where(lane == 127, ends, pltpu.roll(row, 127, 1))
        return [
            taps_ref[3 * r] * left + taps_ref[3 * r + 1] * row + taps_ref[3 * r + 2] * right
            for r in range(3)
        ]

    def put(y, value):
        value = value.astype(BF)
        out_ref[y, 0:chans, :] = value

    h0 = taps(0, edge_ref[0])
    h1 = taps(1, state_ref[0])

    def conv(i, carry):
        older, newer = carry
        h = taps(i, state_ref[i - 1])
        put(i - 2, older + h[2])
        return newer + h[1], h[0]

    older, newer = lax.fori_loop(2, height + 1, conv, (h0[0] + h1[1], h1[0]))
    h = taps(height + 1, edge_ref[1])
    put(height - 1, older + h[2])

    column = lax.broadcasted_iota(jnp.int32, (LANES, GROUP * 128), 0).astype(F32).astype(BF)
    pairs = height // 2
    for f, (low, high) in enumerate(bounds):
        width = high - low
        count = count_ref[f]
        acc_ref[...] = jnp.zeros_like(acc_ref)

        def step(j, _):
            vals, high_of, low_of = [], [], []
            for b in range(GROUP):
                at = order_ref[f, j * GROUP + b]
                vals.append(got_ref[at, low:high, :])
                meta = got_ref[at, META:, :].astype(F32)
                live = j * GROUP + b < count
                high_of.append(jnp.where(live, meta[2 * f : 2 * f + 1], -1.0))
                low_of.append(jnp.where(live, meta[2 * f + 1 : 2 * f + 2], -1.0))
            vals = jnp.concatenate(vals, axis=1)
            high_of = jnp.concatenate(high_of, axis=1)
            low_of = jnp.concatenate(low_of, axis=1)
            hit = jnp.broadcast_to(low_of, (LANES, GROUP * 128)).astype(BF) == column
            onehot = jnp.where(hit, jnp.ones((), BF), jnp.zeros((), BF))
            wanted = jnp.broadcast_to(high_of, (width, GROUP * 128)).astype(BF)
            for first in range(0, pairs, 8):
                lhs = jnp.concatenate(
                    [
                        jnp.where(wanted == jnp.asarray(first + q, BF), vals, jnp.zeros((), BF))
                        for q in range(8)
                    ],
                    axis=0,
                )
                acc_ref[first * width : (first + 8) * width, :] += lax.dot_general(
                    lhs, onehot, (((1,), (1,)), ((), ())), preferred_element_type=F32
                )
            return 0

        lax.fori_loop(0, (count + GROUP - 1) // GROUP, step, 0)
        begin = outs[f]
        for q in range(pairs):
            piece = acc_ref[q * width : (q + 1) * width, :].astype(BF)
            out_ref[2 * q, begin : begin + width, :] = piece[:, :128]
            out_ref[2 * q + 1, begin : begin + width, :] = piece[:, 128:]


def mix_kernel(ca, co, in_ref, coup_a, vec_a, exp_a, eb_a, proj_a, coup_o, vec_o, exp_o, eb_o, proj_o, out_ref):
    rows = in_ref.shape[0]
    half_a, half_o = ca // 2, co // 2
    part = half_a + half_o
    whole = 2 * part

    def lanes(low, size):
        return jnp.concatenate(
            [
                jnp.concatenate(
                    [in_ref[y, low : low + size, :], in_ref[y, whole + low : whole + low + size, :]], axis=0
                )
                for y in range(rows)
            ],
            axis=1,
        )

    def unit(conv, coupled, coup, vec, expand, bias, project):
        mixed = conv.astype(F32) + jnp.dot(coup[...], coupled, preferred_element_type=F32)
        mean = jnp.mean(mixed, axis=0, keepdims=True)
        centred = mixed - mean
        var = jnp.mean(centred * centred, axis=0, keepdims=True)
        normed = (centred * lax.rsqrt(var + 1e-6) * vec[:, 0:1] + vec[:, 1:2]).astype(BF)
        hidden = jnp.dot(expand[...], normed, preferred_element_type=F32) + bias[...]
        hidden = jax.nn.gelu(hidden, approximate=True).astype(BF)
        return jnp.dot(project[...], hidden, preferred_element_type=F32).astype(BF)

    air = unit(lanes(0, half_a), lanes(part, half_o), coup_a, vec_a, exp_a, eb_a, proj_a)
    sea = unit(lanes(half_a, half_o), lanes(part + half_o, half_a), coup_o, vec_o, exp_o, eb_o, proj_o)
    for y in range(rows):
        at = slice(y * 128, (y + 1) * 128)
        for side in range(2):
            base = side * part
            out_ref[y, base : base + half_a, :] = air[side * half_a : (side + 1) * half_a, at]
            out_ref[y, base + half_a : base + part, :] = sea[side * half_o : (side + 1) * half_o, at]


def slots_of(heading):
    lanes = heading[:, 0]
    n = lanes.shape[0]
    i = jnp.arange(n, dtype=jnp.int32)
    before = (lanes[:, None] == lanes[None, :]) & (i[None, :] < i[:, None])
    return lanes * SLOTS + jnp.sum(before.astype(jnp.int32), axis=1)


def compact(valid):
    n = valid.shape[0]
    i = jnp.arange(n, dtype=jnp.int32)
    where = jnp.sum((valid[None, :] & (i[None, :] < i[:, None])).astype(jnp.int32), axis=1)
    at = (i // SLOTS) * (SLOTS + 1) + i % SLOTS
    chosen = valid[None, :] & (where[None, :] == i[:, None])
    return jnp.sum(jnp.where(chosen, at[None, :], 0), axis=1), jnp.sum(valid.astype(jnp.int32))


def local(
    atm, sea, atm_kernel, atm_coupling, atm_gain, atm_shift, atm_expand, atm_expand_bias, atm_project,
    sea_kernel, sea_coupling, sea_gain, sea_shift, sea_expand, sea_expand_bias, sea_project,
    flux_source, flux_target, flux_weight, flux_heading, sst_source, sst_target, sst_weight, sst_heading,
):
    n_tiles, n_rows = lax.axis_size("tiles"), lax.axis_size("rows")
    band = lax.axis_index("tiles")
    last = n_tiles - 1
    half_a, half_o = atm.shape[0], sea.shape[0]
    part = half_a + half_o
    height, width = atm.shape[1], atm.shape[2]
    blocks = flux_source.shape[0]
    bounds = ((0, half_a), (half_a, part))
    params = functools.partial(pltpu.CompilerParams, vmem_limit_bytes=VMEM_LIMIT)
    vmem = pl.BlockSpec(memory_space=pltpu.VMEM)
    smem = pl.BlockSpec(memory_space=pltpu.SMEM)

    state = jnp.transpose(jnp.concatenate([atm, sea], axis=0), (1, 0, 2))

    def fit(a):
        return jnp.pad(a, ((0, 128 - a.shape[0]), (0, 128 - a.shape[1])))

    south_row, north_row = fit(state[0]), fit(state[height - 1])
    west_col, east_col = fit(state[:, :, 0].T), fit(state[:, :, width - 1].T)
    halo = jnp.stack(
        [south_row, south_row, south_row, west_col, west_col, east_col, north_row, north_row, north_row]
    )
    slots = jnp.stack([slots_of(flux_heading), slots_of(sst_heading)])
    source = jnp.stack([flux_source, sst_source])
    target = jnp.stack([flux_target, sst_target])
    weight = jnp.stack([flux_weight, sst_weight])

    def paired(a):
        return a.astype(F32).reshape(2, blocks // 2, 1, 2 * 128)

    meta = jnp.stack([target // LANES, target % LANES], axis=1).astype(F32)[:, :, :, None, :]
    packed = pl.pallas_call(
        functools.partial(pack_kernel, bounds),
        out_shape=jax.ShapeDtypeStruct((9, SLOTS + 1, 128, 128), BF),
        in_specs=[smem] + [vmem] * 6,
        out_specs=vmem,
        compiler_params=params(),
        name="pack",
    )(slots, state, halo, paired(source % LANES), paired(source // LANES), paired(weight), meta)

    got = pl.pallas_call(
        functools.partial(send_kernel, n_tiles, n_rows),
        out_shape=jax.ShapeDtypeStruct((10, SLOTS + 1, 128, 128), BF),
        in_specs=[pl.BlockSpec(memory_space=pl.ANY)],
        out_specs=pl.BlockSpec(memory_space=pl.ANY),
        scratch_shapes=[
            pltpu.SemaphoreType.DMA((9,)),
            pltpu.SemaphoreType.DMA((9,)),
            pltpu.SemaphoreType.DMA,
        ],
        compiler_params=params(collective_id=0, has_side_effects=True),
        name="send",
    )(packed)

    edge = got[:, SLOTS]
    first_band, last_band = band == 0, band == last
    is_air = (jnp.arange(part) < half_a)[:, None]
    south = jnp.where(first_band, 0, edge[7, :part])
    south_w = jnp.where(first_band, 0, edge[8, :part, 127:128])
    south_e = jnp.where(first_band, 0, edge[6, :part, 0:1])

    def across(side):
        perm = [(s, n_rows - 1 - (s + side) % n_rows) for s in range(n_rows)]
        row = state[height - 1]
        if all(a == b for a, b in perm):
            return row
        return lax.ppermute(row, "rows", perm)

    fold = edge[9, :part, ::-1]
    north = jnp.where(last_band, jnp.where(is_air, 0, fold), edge[1, :part])
    north_w = jnp.where(last_band, jnp.where(is_air, 0, across(-1)[:, 0:1]), edge[2, :part, 127:128])
    north_e = jnp.where(last_band, jnp.where(is_air, 0, across(1)[:, 127:128]), edge[0, :part, 0:1])
    zeros = jnp.zeros((part, 128 - height - 2), BF)
    cols = jnp.concatenate(
        [south_w, edge[5, :part, :height], north_w, zeros, south_e, edge[3, :part, :height], north_e, zeros],
        axis=1,
    )
    edges = jnp.stack([south, north])
    taps = jnp.concatenate([atm_kernel, sea_kernel], axis=0).reshape(part, 9).T[:, :, None]
    taps = jnp.broadcast_to(taps, (9, part, 128))

    k = jnp.arange(10)
    usable = jnp.where(k < 3, ~last_band, jnp.where(k < 6, True, jnp.where(k < 9, ~first_band, last_band)))
    listed = got[:, :SLOTS, META : META + 4, 0]
    orders, counts = [], []
    for f in range(2):
        order, count = compact(((listed[:, :, 2 * f] >= 0) & usable[:, None]).reshape(-1))
        orders.append(order)
        counts.append(count)
    mixed_in = pl.pallas_call(
        functools.partial(land_kernel, bounds, (part + half_o, part)),
        out_shape=jax.ShapeDtypeStruct((height, 2 * part, 128), BF),
        in_specs=[smem, smem] + [vmem] * 5,
        out_specs=vmem,
        scratch_shapes=[pltpu.VMEM((height // 2 * half_a, LANES), F32)],
        compiler_params=params(),
        name="land",
    )(
        jnp.stack(orders), jnp.stack(counts), got.reshape(10 * (SLOTS + 1), 128, 128), state, edges, cols, taps
    )

    full = lax.all_to_all(mixed_in, "comp", split_axis=0, concat_axis=1, tiled=True)
    ca, co = 2 * half_a, 2 * half_o
    rows = 4

    def whole(a):
        return pl.BlockSpec(a.shape, lambda i: (0,) * a.ndim)

    weights = [
        atm_coupling, jnp.stack([atm_gain, atm_shift], axis=1), atm_expand, atm_expand_bias[:, None], atm_project,
        sea_coupling, jnp.stack([sea_gain, sea_shift], axis=1), sea_expand, sea_expand_bias[:, None], sea_project,
    ]
    update = pl.pallas_call(
        functools.partial(mix_kernel, ca, co),
        grid=(height // 2 // rows,),
        out_shape=jax.ShapeDtypeStruct((height // 2, 2 * part, 128), BF),
        in_specs=[pl.BlockSpec((rows, 4 * part, 128), lambda i: (i, 0, 0))] + [whole(a) for a in weights],
        out_specs=pl.BlockSpec((rows, 2 * part, 128), lambda i: (i, 0, 0)),
        compiler_params=params(),
        name="mix",
    )(full, *weights)
    update = lax.all_to_all(update, "comp", split_axis=1, concat_axis=0, tiled=True)
    total = jnp.transpose((state.astype(F32) + update.astype(F32)).astype(BF), (1, 0, 2))
    return total[:half_a], total[half_a:]


def solution(mesh):
    grid = P(("groups", "comp"), "tiles", "rows")
    lists = P(("tiles", "rows"), None)
    taps = P("comp", None, None)
    placed = (grid, grid, taps) + (P(),) * 6 + (taps,) + (P(),) * 6 + (lists,) * 8
    return jax.shard_map(local, mesh=mesh, in_specs=placed, out_specs=(grid, grid), check_vma=False)
```

time: 615 us -> 249 us (0.40)
  the two profiles are of different devices: /device:TPU:29 before, /device:TPU:9 now
where the time goes in v1:
time: 249 us; the launch traced here: 248 us
  Pallas kernels  158 us (63%)
  local copies, waits for them, and re-layouts  59.8 us (24%)
  other arithmetic  15.5 us (6%)
  blocking collectives  13.3 us (5%)
    pallas_call x1, Pallas kernels, local(): pl.pallas_call(functools.partial(send_kernel, n_tiles, n_rows), out_shape...  75.6 us
    pallas_call x1, Pallas kernels, local(): pl.pallas_call(functools.partial(land_kernel, bounds, (part + half_o, par...  43.8 us
    pallas_call x1, Pallas kernels, local(): pl.pallas_call(functools.partial(pack_kernel, bounds), out_shape=jax.Shap...  26.7 us
    unnamed x55, local copies, waits for them, and re-layouts  13.1 us
    slice x3, local copies, waits for them, and re-layouts, local(): south_row, north_row = (fit(state[0]), fit(state[height - 1]))  12.7 us
    pallas_call x1, Pallas kernels, local(): pl.pallas_call(functools.partial(mix_kernel, ca, co), grid=(height // 2 /...  12.2 us
    convert_element_type x2, local copies, waits for them, and re-layouts, local(): update.astype(F32)  10.9 us
    transpose x1, local copies, waits for them, and re-layouts, local(): state = jnp.transpose(jnp.concatenate([atm, sea], axis=0), (1, 0, 2))  8.36 us

profile of v1, /device:TPU:9, one launch (start us, length us, event | category | flops | bytes accessed | tf_op | source)
XLA Modules:
  0.0 248.0 jit_solution(5157547730831942563)
XLA Ops:
  0.6 4.0 %copy.149 = bf16[64,64,128]{1,0,2:T(8,128)(2,1)S(1)} copy(bf16[64,64,128]{2,1,0:T(8,128)(2,1)} %param.24) | data formatting | bytes 2097152 | tf_op args[0]
  4.7 1.8 copy.150
  6.5 2.2 maximum_bitcast_fusion
  8.6 4.2 %fusion.22 = (bf16[1,112,128]{0,1,2:T(8,128)(2,1)}, bf16[1,112,128]{0,1,2:T(8,128)(2,1)}) fusion(bf16[64,112,128]{0,1,2:T(8,128)(2,1)S(1)} %maximum_bitcast_fusion), kind=kLoop, calls=%fused_computation.94 | loop fusion | bytes 114688 | tf_op jit(solution)/shard_map/slice | solution.py:293
  12.9 8.4 %copy.154.state_ref = bf16[64,112,128]{2,1,0:T(8,128)(2,1)} copy(bf16[64,112,128]{0,1,2:T(8,128)(2,1)} %copy-done) | data formatting | bytes 3670016 | tf_op jit(solution)/shard_map/transpose | solution.py:288
  21.3 4.3 %copy.151 = bf16[1,112,128]{2,1,0:T(8,128)(2,1)S(1)} copy(bf16[1,112,128]{0,1,2:T(8,128)(2,1)} %get-tuple-element.25) | data formatting | bytes 57344 | tf_op jit(solution)/shard_map/slice | solution.py:293
  25.7 4.2 %copy.152 = bf16[1,112,128]{2,1,0:T(8,128)(2,1)S(1)} copy(bf16[1,112,128]{0,1,2:T(8,128)(2,1)} %get-tuple-element.24) | data formatting | bytes 57344 | tf_op jit(solution)/shard_map/slice | solution.py:293
  34.1 26.7 %pack.1.packed_ref = bf16[9,17,128,128]{3,2,1,0:T(8,128)(2,1)} custom-call(s32[2,64]{1,0:T(2,128)} %pad_add_fusion.3.slots_ref, bf16[64,112,128]{2,1,0:T(8,128)(2,1)} %copy.154.state_ref, bf16[9,128,128]{2,1,0:T(8,128)(2,1)} %copy-done.3, f32[2,32,1,256]{3,2,1,0:T(1,128)} %fusion.5.pos_ref, f32[2,32,1,256]{3,2,1,0:T(1,128)} %get-tuple-element.22.high_ref, ...), custom_call_target="tpu_custom_call" | custom-call | tf_op jit(solution)/shard_map/pack/pallas_call | solution.py:307
  60.8 75.6 %send.1 = bf16[10,17,128,128]{3,2,1,0:T(8,128)(2,1)} custom-call(bf16[9,17,128,128]{3,2,1,0:T(8,128)(2,1)} %pack.1.packed_ref), custom_call_target="tpu_custom_call" | custom-call | tf_op jit(solution)/shard_map/send/pallas_call | solution.py:316
  136.5 1.0 slice_bitcast_fusion
  137.5 1.0 slice.69
  141.5 2.0 pad_add_fusion.4.count_ref
  146.0 43.8 %land.1 = bf16[64,224,128]{2,1,0:T(8,128)(2,1)} custom-call(s32[2,160]{1,0:T(2,128)} %pad_add_fusion.2.order_ref, s32[2]{0:T(128)} %pad_add_fusion.4.count_ref, bf16[170,128,128]{2,1,0:T(8,128)(2,1)} %bitcast.101, bf16[64,112,128]{2,1,0:T(8,128)(2,1)} %copy.154.state_ref, bf16[2,112,128]{2,1,0:T(8,128)(2,1)} %pad_maximum_fusion.1.edge_ref, ...), custom_call_target="tpu_custom_call" | custom-call | tf_op jit(solution)/shard_map/land/pallas_call | solution.py:365
  189.8 8.1 %all_to_all.27 = bf16[64,224,128]{2,1,0:T(8,128)(2,1)S(1)} all-to-all(bf16[64,224,128]{2,1,0:T(8,128)(2,1)} %land.1), channel_id=1, replica_groups=mesh['groups'=2,'tiles'=4,'rows'=2,'comp'=2] {'comp'}, dimensions={0} | all-to-all | bytes 7340032 | tf_op jit(solution)/shard_map/all_to_all | solution.py:377
  198.0 2.2 copy.162
  204.0 12.2 %mix.1 = bf16[32,224,128]{2,1,0:T(8,128)(2,1)} custom-call(bf16[32,448,128]{2,1,0:T(8,128)(2,1)} %bitcast.103, bf16[128,96]{1,0:T(8,128)(2,1)} %copy.163.coup_a, f32[128,2]{1,0:T(8,128)} %copy.164.vec_a, bf16[256,128]{1,0:T(8,128)(2,1)} %exp_a.1, f32[256,1]{1,0:T(8,128)} %copy.165.eb_a, bf16[128,256]{1,0:T(8,128)(2,1)} %proj_a.1, bf16[96,128]{1,0:T(8,128)(2,1)} %coup_o.1, ...), custom_call_target="tpu_custom_call" | custom-call | tf_op jit(solution)/shard_map/mix/pallas_call | solution.py:388
  216.1 2.2 copy.168
  218.3 5.2 %all_to_all.28 = bf16[32,224,128]{2,0,1:T(8,128)(2,1)S(1)} all-to-all(bf16[32,224,128]{2,0,1:T(8,128)(2,1)S(1)} %copy.168), channel_id=1, replica_groups=mesh['groups'=2,'tiles'=4,'rows'=2,'comp'=2] {'comp'}, dimensions={1} | all-to-all | bytes 3670016 | tf_op jit(solution)/shard_map/all_to_all | solution.py:397
  224.7 2.2 copy.170
  226.9 8.8 %copy.171 = f32[64,112,128]{0,1,2:T(8,128)} copy(f32[64,112,128]{2,1,0:T(8,128)} %bitcast.104) | data formatting | bytes 7340032 | tf_op jit(solution)/shard_map/convert_element_type | solution.py:398
  235.6 4.0 %fusion = bf16[112,64,128]{1,0,2:T(8,128)(2,1)S(1)} fusion(f32[64,112,128]{0,1,2:T(8,128)} %copy.171, bf16[48,64,128]{1,0,2:T(8,128)(2,1)} %copy.150, bf16[64,64,128]{1,0,2:T(8,128)(2,1)S(1)} %copy.149), kind=kLoop, calls=%fused_computation.1 | loop fusion | flops 6422528 | bytes 7340032 | tf_op jit(solution)/shard_map/transpose | solution.py:398
  239.7 1.8 slice.103
  242.2 4.1 %copy.172 = bf16[64,64,128]{2,1,0:T(8,128)(2,1)} copy(bf16[64,64,128]{1,0,2:T(8,128)(2,1)} %slice.103) | data formatting | bytes 2097152
  246.3 1.7 copy.173
  (99 shorter events, 15.2 us)
Async XLA Ops:
  0.6 4.0 %copy-start.2 = (bf16[48,64,128]{2,1,0:T(8,128)(2,1)S(1)}, bf16[48,64,128]{2,1,0:T(8,128)(2,1)}, u32[]{:S(2)}) copy-start(bf16[48,64,128]{2,1,0:T(8,128)(2,1)} %param.25) | copy-start | bytes 2359300
  8.6 4.2 %copy-start = (bf16[64,112,128]{0,1,2:T(8,128)(2,1)}, bf16[64,112,128]{0,1,2:T(8,128)(2,1)S(1)}, u32[]{:S(2)}) copy-start(bf16[64,112,128]{0,1,2:T(8,128)(2,1)S(1)} %maximum_bitcast_fusion) | copy-start | bytes 5505028
  21.2 8.7 %copy-start.15 = (s32[64,1]{0,1:T(1,128)S(1)}, s32[64,1]{0,1:T(1,128)}, u32[]{:S(2)}) copy-start(s32[64,1]{0,1:T(1,128)} %param.47) | copy-start | bytes 772
  21.2 8.9 %copy-start.16 = (s32[64,1]{0,1:T(1,128)S(1)}, s32[64,1]{0,1:T(1,128)}, u32[]{:S(2)}) copy-start(s32[64,1]{0,1:T(1,128)} %param.43) | copy-start | bytes 772
  21.2 9.1 %copy-start.4 = (s32[64,128]{1,0:T(8,128)S(1)}, s32[64,128]{1,0:T(8,128)}, u32[]{:S(2)}) copy-start(s32[64,128]{1,0:T(8,128)} %param.44) | copy-start | bytes 98308
  21.2 9.1 %copy-start.5 = (s32[64,128]{1,0:T(8,128)S(1)}, s32[64,128]{1,0:T(8,128)}, u32[]{:S(2)}) copy-start(s32[64,128]{1,0:T(8,128)} %param.40) | copy-start | bytes 98308
  21.3 10.8 %copy-start.6 = (s32[64,128]{1,0:T(8,128)S(1)}, s32[64,128]{1,0:T(8,128)}, u32[]{:S(2)}) copy-start(s32[64,128]{1,0:T(8,128)} %param.45) | copy-start | bytes 98308
  21.3 10.7 %copy-start.7 = (s32[64,128]{1,0:T(8,128)S(1)}, s32[64,128]{1,0:T(8,128)}, u32[]{:S(2)}) copy-start(s32[64,128]{1,0:T(8,128)} %param.41) | copy-start | bytes 98308
  21.3 12.2 %copy-start.8 = (f32[64,128]{1,0:T(8,128)S(1)}, f32[64,128]{1,0:T(8,128)}, u32[]{:S(2)}) copy-start(f32[64,128]{1,0:T(8,128)} %param.46) | copy-start | bytes 98308
  21.3 12.1 %copy-start.9 = (f32[64,128]{1,0:T(8,128)S(1)}, f32[64,128]{1,0:T(8,128)}, u32[]{:S(2)}) copy-start(f32[64,128]{1,0:T(8,128)} %param.42) | copy-start | bytes 98308
  30.0 4.2 %copy-start.3 = (bf16[9,128,128]{2,1,0:T(8,128)(2,1)}, bf16[9,128,128]{2,1,0:T(8,128)(2,1)S(1)}, u32[]{:S(2)}) copy-start(bf16[9,128,128]{2,1,0:T(8,128)(2,1)S(1)} %bitcast_dynamic-update-slice_fusion.2.halo_ref) | copy-start | bytes 884740
  60.8 79.1 %copy-start.11 = (f32[48,3,3]{0,2,1:T(4,128)S(1)}, f32[48,3,3]{0,2,1:T(4,128)}, u32[]{:S(2)}) copy-start(f32[48,3,3]{0,2,1:T(4,128)} %param.33) | copy-start | bytes 5188
  60.8 79.1 %copy-start.12 = (f32[64,3,3]{0,2,1:T(4,128)S(1)}, f32[64,3,3]{0,2,1:T(4,128)}, u32[]{:S(2)}) copy-start(f32[64,3,3]{0,2,1:T(4,128)} %param.26) | copy-start | bytes 6916
  197.9 2.2 copy-start.13
  197.9 3.0 %copy-start.14 = (f32[192]{0:T(256)S(1)}, f32[192]{0:T(256)}, u32[]{:S(2)}) copy-start(f32[192]{0:T(256)} %param.38) | copy-start | bytes 2308
  197.9 3.8 %copy-start.17 = (f32[128]{0:T(128)S(1)}, f32[128]{0:T(128)}, u32[]{:S(2)}) copy-start(f32[128]{0:T(128)} %param.29) | copy-start | bytes 1540
  197.9 3.8 %copy-start.18 = (f32[128]{0:T(128)S(1)}, f32[128]{0:T(128)}, u32[]{:S(2)}) copy-start(f32[128]{0:T(128)} %param.28) | copy-start | bytes 1540
  197.9 4.6 %copy-start.19 = (f32[96]{0:T(128)S(1)}, f32[96]{0:T(128)}, u32[]{:S(2)}) copy-start(f32[96]{0:T(128)} %param.36) | copy-start | bytes 1156
  197.9 4.6 %copy-start.20 = (f32[96]{0:T(128)S(1)}, f32[96]{0:T(128)}, u32[]{:S(2)}) copy-start(f32[96]{0:T(128)} %param.35) | copy-start | bytes 1156
  197.9 5.3 %copy-start.10 = (bf16[128,96]{0,1:T(8,128)(2,1)S(1)}, bf16[128,96]{0,1:T(8,128)(2,1)}, u32[]{:S(2)}) copy-start(bf16[128,96]{0,1:T(8,128)(2,1)} %param.27) | copy-start | bytes 73732
  239.7 2.5 copy-start.1
  242.2 4.1 %slice-start = ((bf16[112,64,128]{1,0,2:T(8,128)(2,1)}), bf16[48,64,128]{1,0,2:T(8,128)(2,1)S(1)}, s32[]{:S(2)}) async-start(bf16[112,64,128]{1,0,2:T(8,128)(2,1)} %copy-done.1), calls=%async_computation.2 | async-start | bytes 3145728 | tf_op jit(solution)/shard_map/slice | solution.py:399

commit v2 on v1

--- a/solution.py
+++ b/solution.py
@@ -17,17 +17,38 @@
 MESH = pl.DeviceIdType.MESH
 
 
-def pack_kernel(bounds, slots_ref, state_ref, halo_ref, pos_ref, high_ref, weight_ref, meta_ref, out_ref):
-    flat_slots = SLOTS + 1
-    pairs = state_ref.shape[0] // 2
+def pack_kernel(bounds, slots_ref, atm_ref, sea_ref, pos_ref, high_ref, weight_ref, meta_ref, out_ref, state_ref):
+    height = state_ref.shape[0]
+    chans_all = state_ref.shape[1]
+    pairs = height // 2
+    for field, (low, high) in zip((atm_ref, sea_ref), bounds):
+        for y in range(0, height, 16):
+            state_ref[y : y + 16, low:high, :] = jnp.swapaxes(field[:, y : y + 16, :], 0, 1)
 
     def clear(i, _):
         out_ref[i // SLOTS, lax.rem(i, SLOTS), META:, :] = jnp.full((16, 128), -1, BF)
         return 0
 
     lax.fori_loop(0, 9 * SLOTS, clear, 0)
+
+    row_at = lax.broadcasted_iota(jnp.int32, (128, LANES), 0)
+    lane_at = lax.broadcasted_iota(jnp.int32, (128, LANES), 1)
+
+    def column_of(y, total):
+        pick = ((row_at == 0) & (lane_at == y)) | ((row_at == 127) & (lane_at == y + 128))
+        return total + jnp.dot(state_ref[y], pick.astype(F32).astype(BF), preferred_element_type=F32)
+
+    columns = lax.fori_loop(0, height, column_of, jnp.zeros((chans_all, LANES), F32)).astype(BF)
     for k in range(9):
-        out_ref[k, flat_slots - 1] = halo_ref[k]
+        if k // 3 == 0:
+            out_ref[k, SLOTS, :chans_all, :] = state_ref[0]
+        elif k // 3 == 2:
+            out_ref[k, SLOTS, :chans_all, :] = state_ref[height - 1]
+        elif k == 3:
+            out_ref[k, SLOTS, :chans_all, :] = columns[:, :128]
+        elif k == 5:
+            out_ref[k, SLOTS, :chans_all, :] = columns[:, 128:]
+
     column = lax.broadcasted_iota(jnp.int32, (LANES, LANES), 0).astype(F32).astype(BF)
     row16 = lax.broadcasted_iota(jnp.int32, (16, 128), 0)
 
@@ -132,33 +153,67 @@
             copy(i).wait_recv()
 
 
-def land_kernel(
-    bounds, outs, order_ref, count_ref, got_ref, state_ref, edge_ref, cols_ref, taps_ref,
-    out_ref, acc_ref,
-):
+def land_kernel(bounds, outs, flags_ref, got_ref, state_ref, across_ref, taps_ref, out_ref, acc_ref, order_ref):
     height = state_ref.shape[0]
     chans = state_ref.shape[1]
+    stride = SLOTS + 1
+    first_band, last_band = flags_ref[0] == 1, flags_ref[1] == 1
     row_of = lax.broadcasted_iota(jnp.int32, (256, 128), 0)
     lane_of = lax.broadcasted_iota(jnp.int32, (256, 128), 1)
     lane = lax.broadcasted_iota(jnp.int32, (chans, 128), 1)
-    cols = cols_ref[...]
+    is_air = lax.broadcasted_iota(jnp.int32, (chans, 128), 0) < bounds[0][1]
+
+    def edge(k):
+        return got_ref[k * stride + SLOTS, :chans, :]
+
+    cols = jnp.concatenate([edge(5), edge(3)], axis=1)
+    wide = lax.broadcasted_iota(jnp.int32, (chans, 256), 1) % 128
+    cols = jnp.where(wide < height, cols.astype(F32), 0.0).astype(BF)
+
+    def spread(row, left, right):
+        return [
+            taps_ref[3 * r] * left + taps_ref[3 * r + 1] * row + taps_ref[3 * r + 2] * right
+            for r in range(3)
+        ]
 
     def taps(i, row):
-        pick = ((row_of == i) & (lane_of == 0)) | ((row_of == i + 128) & (lane_of == 127))
+        y = i - 1
+        pick = ((row_of == y) & (lane_of == 0)) | ((row_of == y + 128) & (lane_of == 127))
         ends = jnp.dot(cols, pick.astype(F32).astype(BF), preferred_element_type=F32)
         row = row.astype(F32)
         left = jnp.where(lane == 0, ends, pltpu.roll(row, 1, 1))
         right = jnp.where(lane == 127, ends, pltpu.roll(row, 127, 1))
-        return [
-            taps_ref[3 * r] * left + taps_ref[3 * r + 1] * row + taps_ref[3 * r + 2] * right
-            for r in range(3)
-        ]
+        return spread(row, left, right)
+
+    def beyond(row, west, east):
+        left = jnp.where(lane == 0, west, pltpu.roll(row, 1, 1))
+        right = jnp.where(lane == 127, east, pltpu.roll(row, 127, 1))
+        return row, left, right
+
+    def row_from(middle, west, east):
+        return beyond(
+            edge(middle).astype(F32),
+            pltpu.roll(edge(west).astype(F32), 1, 1),
+            pltpu.roll(edge(east).astype(F32), 127, 1),
+        )
+
+    south = [jnp.where(first_band, 0.0, part) for part in row_from(7, 8, 6)]
+    flip_row = lax.broadcasted_iota(jnp.int32, (128, 128), 0)
+    flip_lane = lax.broadcasted_iota(jnp.int32, (128, 128), 1)
+    flip = (flip_row + flip_lane == 127).astype(F32).astype(BF)
+    fold = jnp.where(last_band, edge(9).astype(F32), 0.0).astype(BF)
+    fold = jnp.dot(fold, flip, preferred_element_type=F32)
+    folded = beyond(fold, across_ref[0].astype(F32), across_ref[1].astype(F32))
+    north = [
+        jnp.where(last_band, jnp.where(is_air, 0.0, over), part)
+        for over, part in zip(folded, row_from(1, 2, 0))
+    ]
 
     def put(y, value):
         value = value.astype(BF)
         out_ref[y, 0:chans, :] = value
 
-    h0 = taps(0, edge_ref[0])
+    h0 = spread(*south)
     h1 = taps(1, state_ref[0])
 
     def conv(i, carry):
@@ -168,20 +223,39 @@
         return newer + h[1], h[0]
 
     older, newer = lax.fori_loop(2, height + 1, conv, (h0[0] + h1[1], h1[0]))
-    h = taps(height + 1, edge_ref[1])
+    h = spread(*north)
     put(height - 1, older + h[2])
 
     column = lax.broadcasted_iota(jnp.int32, (LANES, GROUP * 128), 0).astype(F32).astype(BF)
     pairs = height // 2
+    place_row = lax.broadcasted_iota(jnp.int32, (16, 128), 0)
+    place_lane = lax.broadcasted_iota(jnp.int32, (16, 128), 1)
+    counts = [jnp.int32(0), jnp.int32(0)]
+    for k in range(10):
+        places = got_ref[k * stride : k * stride + SLOTS, META:, :].astype(F32)
+        filled = jnp.sum((places >= 0).astype(F32), axis=0)
+        usable = True if 3 <= k < 6 else jnp.logical_not(last_band) if k < 3 else jnp.logical_not(first_band) if k < 9 else last_band
+        for f in range(2):
+            there = (place_row == 2 * f) & (place_lane == 0)
+            count = jnp.sum(jnp.where(there, filled, 0.0)).astype(jnp.int32)
+            count = jnp.where(usable, count, 0)
+            base = counts[f]
+
+            def note(i, _):
+                order_ref[f, base + i] = k * stride + i
+                return 0
+
+            lax.fori_loop(0, count, note, 0)
+            counts[f] = base + count
     for f, (low, high) in enumerate(bounds):
         width = high - low
-        count = count_ref[f]
+        count = counts[f]
         acc_ref[...] = jnp.zeros_like(acc_ref)
 
         def step(j, _):
             vals, high_of, low_of = [], [], []
             for b in range(GROUP):
-                at = order_ref[f, j * GROUP + b]
+                at = order_ref[f, jnp.minimum(j * GROUP + b, count - 1)]
                 vals.append(got_ref[at, low:high, :])
                 meta = got_ref[at, META:, :].astype(F32)
                 live = j * GROUP + b < count
@@ -215,17 +289,14 @@
 
 
 def mix_kernel(ca, co, in_ref, coup_a, vec_a, exp_a, eb_a, proj_a, coup_o, vec_o, exp_o, eb_o, proj_o, out_ref):
-    rows = in_ref.shape[0]
+    rows = in_ref.shape[1]
     half_a, half_o = ca // 2, co // 2
     part = half_a + half_o
-    whole = 2 * part
 
     def lanes(low, size):
         return jnp.concatenate(
             [
-                jnp.concatenate(
-                    [in_ref[y, low : low + size, :], in_ref[y, whole + low : whole + low + size, :]], axis=0
-                )
+                jnp.concatenate([in_ref[0, y, low : low + size, :], in_ref[1, y, low : low + size, :]], axis=0)
                 for y in range(rows)
             ],
             axis=1,
@@ -246,9 +317,14 @@
     for y in range(rows):
         at = slice(y * 128, (y + 1) * 128)
         for side in range(2):
-            base = side * part
-            out_ref[y, base : base + half_a, :] = air[side * half_a : (side + 1) * half_a, at]
-            out_ref[y, base + half_a : base + part, :] = sea[side * half_o : (side + 1) * half_o, at]
+            out_ref[side, y, :half_a, :] = air[side * half_a : (side + 1) * half_a, at]
+            out_ref[side, y, half_a:part, :] = sea[side * half_o : (side + 1) * half_o, at]
+
+
+def finish_kernel(bounds, update_ref, atm_ref, sea_ref, atm_out, sea_out):
+    for field, out, (low, high) in zip((atm_ref, sea_ref), (atm_out, sea_out), bounds):
+        update = jnp.swapaxes(update_ref[:, low:high, :], 0, 1)
+        out[...] = (field[...].astype(F32) + update.astype(F32)).astype(BF)
 
 
 def slots_of(heading):
@@ -257,15 +333,6 @@
     i = jnp.arange(n, dtype=jnp.int32)
     before = (lanes[:, None] == lanes[None, :]) & (i[None, :] < i[:, None])
     return lanes * SLOTS + jnp.sum(before.astype(jnp.int32), axis=1)
-
-
-def compact(valid):
-    n = valid.shape[0]
-    i = jnp.arange(n, dtype=jnp.int32)
-    where = jnp.sum((valid[None, :] & (i[None, :] < i[:, None])).astype(jnp.int32), axis=1)
-    at = (i // SLOTS) * (SLOTS + 1) + i % SLOTS
-    chosen = valid[None, :] & (where[None, :] == i[:, None])
-    return jnp.sum(jnp.where(chosen, at[None, :], 0), axis=1), jnp.sum(valid.astype(jnp.int32))
 
 
 def local(
@@ -285,16 +352,6 @@
     vmem = pl.BlockSpec(memory_space=pltpu.VMEM)
     smem = pl.BlockSpec(memory_space=pltpu.SMEM)
 
-    state = jnp.transpose(jnp.concatenate([atm, sea], axis=0), (1, 0, 2))
-
-    def fit(a):
-        return jnp.pad(a, ((0, 128 - a.shape[0]), (0, 128 - a.shape[1])))
-
-    south_row, north_row = fit(state[0]), fit(state[height - 1])
-    west_col, east_col = fit(state[:, :, 0].T), fit(state[:, :, width - 1].T)
-    halo = jnp.stack(
-        [south_row, south_row, south_row, west_col, west_col, east_col, north_row, north_row, north_row]
-    )
     slots = jnp.stack([slots_of(flux_heading), slots_of(sst_heading)])
     source = jnp.stack([flux_source, sst_source])
     target = jnp.stack([flux_target, sst_target])
@@ -304,14 +361,17 @@
         return a.astype(F32).reshape(2, blocks // 2, 1, 2 * 128)
 
     meta = jnp.stack([target // LANES, target % LANES], axis=1).astype(F32)[:, :, :, None, :]
-    packed = pl.pallas_call(
+    packed, state = pl.pallas_call(
         functools.partial(pack_kernel, bounds),
-        out_shape=jax.ShapeDtypeStruct((9, SLOTS + 1, 128, 128), BF),
+        out_shape=[
+            jax.ShapeDtypeStruct((9, SLOTS + 1, 128, 128), BF),
+            jax.ShapeDtypeStruct((height, part, 128), BF),
+        ],
         in_specs=[smem] + [vmem] * 6,
-        out_specs=vmem,
+        out_specs=[vmem, vmem],
         compiler_params=params(),
         name="pack",
-    )(slots, state, halo, paired(source % LANES), paired(source // LANES), paired(weight), meta)
+    )(slots, atm, sea, paired(source % LANES), paired(source // LANES), paired(weight), meta)
 
     got = pl.pallas_call(
         functools.partial(send_kernel, n_tiles, n_rows),
@@ -327,13 +387,6 @@
         name="send",
     )(packed)
 
-    edge = got[:, SLOTS]
-    first_band, last_band = band == 0, band == last
-    is_air = (jnp.arange(part) < half_a)[:, None]
-    south = jnp.where(first_band, 0, edge[7, :part])
-    south_w = jnp.where(first_band, 0, edge[8, :part, 127:128])
-    south_e = jnp.where(first_band, 0, edge[6, :part, 0:1])
-
     def across(side):
         perm = [(s, n_rows - 1 - (s + side) % n_rows) for s in range(n_rows)]
         row = state[height - 1]
@@ -341,40 +394,24 @@
             return row
         return lax.ppermute(row, "rows", perm)
 
-    fold = edge[9, :part, ::-1]
-    north = jnp.where(last_band, jnp.where(is_air, 0, fold), edge[1, :part])
-    north_w = jnp.where(last_band, jnp.where(is_air, 0, across(-1)[:, 0:1]), edge[2, :part, 127:128])
-    north_e = jnp.where(last_band, jnp.where(is_air, 0, across(1)[:, 127:128]), edge[0, :part, 0:1])
-    zeros = jnp.zeros((part, 128 - height - 2), BF)
-    cols = jnp.concatenate(
-        [south_w, edge[5, :part, :height], north_w, zeros, south_e, edge[3, :part, :height], north_e, zeros],
-        axis=1,
-    )
-    edges = jnp.stack([south, north])
     taps = jnp.concatenate([atm_kernel, sea_kernel], axis=0).reshape(part, 9).T[:, :, None]
     taps = jnp.broadcast_to(taps, (9, part, 128))
 
-    k = jnp.arange(10)
-    usable = jnp.where(k < 3, ~last_band, jnp.where(k < 6, True, jnp.where(k < 9, ~first_band, last_band)))
-    listed = got[:, :SLOTS, META : META + 4, 0]
-    orders, counts = [], []
-    for f in range(2):
-        order, count = compact(((listed[:, :, 2 * f] >= 0) & usable[:, None]).reshape(-1))
-        orders.append(order)
-        counts.append(count)
+    flags = jnp.stack([band == 0, band == last]).astype(jnp.int32)
     mixed_in = pl.pallas_call(
         functools.partial(land_kernel, bounds, (part + half_o, part)),
         out_shape=jax.ShapeDtypeStruct((height, 2 * part, 128), BF),
-        in_specs=[smem, smem] + [vmem] * 5,
+        in_specs=[smem] + [vmem] * 4,
         out_specs=vmem,
-        scratch_shapes=[pltpu.VMEM((height // 2 * half_a, LANES), F32)],
+        scratch_shapes=[
+            pltpu.VMEM((height // 2 * half_a, LANES), F32),
+            pltpu.SMEM((2, 10 * SLOTS), jnp.int32),
+        ],
         compiler_params=params(),
         name="land",
-    )(
-        jnp.stack(orders), jnp.stack(counts), got.reshape(10 * (SLOTS + 1), 128, 128), state, edges, cols, taps
-    )
-
-    full = lax.all_to_all(mixed_in, "comp", split_axis=0, concat_axis=1, tiled=True)
+    )(flags, got.reshape(10 * (SLOTS + 1), 128, 128), state, jnp.stack([across(-1), across(1)]), taps)
+
+    full = lax.all_to_all(mixed_in.reshape(2, height // 2, 2 * part, 128), "comp", split_axis=0, concat_axis=0)
     ca, co = 2 * half_a, 2 * half_o
     rows = 4
 
@@ -388,15 +425,28 @@
     update = pl.pallas_call(
         functools.partial(mix_kernel, ca, co),
         grid=(height // 2 // rows,),
-        out_shape=jax.ShapeDtypeStruct((height // 2, 2 * part, 128), BF),
-        in_specs=[pl.BlockSpec((rows, 4 * part, 128), lambda i: (i, 0, 0))] + [whole(a) for a in weights],
-        out_specs=pl.BlockSpec((rows, 2 * part, 128), lambda i: (i, 0, 0)),
+        out_shape=jax.ShapeDtypeStruct((2, height // 2, part, 128), BF),
+        in_specs=[pl.BlockSpec((2, rows, 2 * part, 128), lambda i: (0, i, 0, 0))] + [whole(a) for a in weights],
+        out_specs=pl.BlockSpec((2, rows, part, 128), lambda i: (0, i, 0, 0)),
         compiler_params=params(),
         name="mix",
     )(full, *weights)
-    update = lax.all_to_all(update, "comp", split_axis=1, concat_axis=0, tiled=True)
-    total = jnp.transpose((state.astype(F32) + update.astype(F32)).astype(BF), (1, 0, 2))
-    return total[:half_a], total[half_a:]
+    update = lax.all_to_all(update, "comp", split_axis=0, concat_axis=0).reshape(height, part, 128)
+
+    def band_of(chans):
+        return pl.BlockSpec((chans, 16, 128), lambda i: (0, i, 0))
+
+    return tuple(
+        pl.pallas_call(
+            functools.partial(finish_kernel, bounds),
+            grid=(height // 16,),
+            out_shape=[jax.ShapeDtypeStruct(atm.shape, BF), jax.ShapeDtypeStruct(sea.shape, BF)],
+            in_specs=[pl.BlockSpec((16, part, 128), lambda i: (i, 0, 0)), band_of(half_a), band_of(half_o)],
+            out_specs=[band_of(half_a), band_of(half_o)],
+            compiler_params=params(),
+            name="finish",
+        )(update, atm, sea)
+    )
 
 
 def solution(mesh):

time: 249 us -> 208 us (0.84)
  local copies, waits for them, and re-layouts: 59.8 us -> 5.53 us
  Pallas kernels: 158 us -> 177 us
  starting transfers between devices: 0 us -> 6.03 us
  other arithmetic: 15.5 us -> 9.94 us
  blocking collectives: 13.3 us -> 8.2 us
    pallas_call x1 -> x2, Pallas kernels: 26.7 us -> 41.9 us  [the longest x1 37.5 us: local(): pl.pallas_call(functools.partial(pack_kernel, bounds), out_shape=[jax.Sha...]
    slice x9 -> x1, local copies, waits for them, and re-layouts: 15.9 us -> 0.75 us  [across(): row = state[height - 1]]
    unnamed x55 -> x19, local copies, waits for them, and re-layouts: 13.1 us -> 0.76 us
    convert_element_type x2 -> x0, local copies, waits for them, and re-layouts: 10.9 us -> none  [local(): update.astype(F32)]
    transpose x2 -> x0, local copies, waits for them, and re-layouts: 8.37 us -> none  [the longest x1 8.36 us: local(): state = jnp.transpose(jnp.concatenate([atm, sea], axis=0), (1, 0, 2))]
    transpose x2 -> x0, other arithmetic: 6.18 us -> none  [the longest x1 4.02 us: local(): jnp.transpose((state.astype(F32) + update.astype(F32)).astype(BF), (1, 0,...]
    all_to_all x0 -> x1, starting transfers between devices: none -> 6.03 us  [local(): lax.all_to_all(mixed_in.reshape(2, height // 2, 2 * part, 128), 'comp', s...]
    all_to_all x2 -> x1, blocking collectives: 13.3 us -> 8.2 us  [local(): lax.all_to_all(update, 'comp', split_axis=0, concat_axis=0)]
  transfers between devices with their start and end apart: 0 -> 1, of which waited for: 0 -> 0; matrix products, arithmetic and copies ran while one was open for 0% -> 2% of each run, Pallas kernels for 0% -> 0%
where the time goes in v2:
time: 208 us; the launch traced here: 207 us
  Pallas kernels  177 us (85%)
  other arithmetic  9.94 us (5%)
  blocking collectives  8.2 us (4%)
  starting transfers between devices  6.03 us (3%)
  local copies, waits for them, and re-layouts  5.53 us (3%)
    pallas_call x1, Pallas kernels, local(): pl.pallas_call(functools.partial(send_kernel, n_tiles, n_rows), out_shape...  75.7 us
    pallas_call x1, Pallas kernels, local(): pl.pallas_call(functools.partial(land_kernel, bounds, (part + half_o, par...  46.8 us
    pallas_call x1, Pallas kernels, local(): pl.pallas_call(functools.partial(pack_kernel, bounds), out_shape=[jax.Sha...  37.5 us
    pallas_call x1, Pallas kernels, local(): pl.pallas_call(functools.partial(mix_kernel, ca, co), grid=(height // 2 /...  12.3 us
    all_to_all x1, blocking collectives, local(): lax.all_to_all(update, 'comp', split_axis=0, concat_axis=0)  8.2 us
    all_to_all x1, starting transfers between devices, local(): lax.all_to_all(mixed_in.reshape(2, height // 2, 2 * part, 128), 'comp', s...  6.03 us
    pallas_call x1, Pallas kernels, local(): pl.pallas_call(functools.partial(finish_kernel, bounds), grid=(height //...  4.38 us
  transfers between devices with their start and end apart: 1, of which 0 were waited for; matrix products, arithmetic and copies ran while one was open for 2% of the time, Pallas kernels for 0%

profile of v2, /device:TPU:9, one launch (start us, length us, event | category | flops | bytes accessed | tf_op | source)
XLA Modules:
  0.0 207.2 jit_solution(15030639873580948519)
XLA Ops:
  0.6 0.9 convert_reduce_fusion
  1.5 0.9 convert_reduce_fusion.1
  2.5 1.7 fusion.2
  4.2 0.7 fusion.pos_ref
  4.9 0.7 bitcast_add_fusion
  6.2 1.5 pad_maximum_fusion.weight_ref
  7.6 0.8 add_select_fusion.1
  8.5 0.7 add_convert_fusion.meta_ref
  9.2 37.5 %pack.1 = (bf16[9,17,128,128]{3,2,1,0:T(8,128)(2,1)}, bf16[64,112,128]{2,1,0:T(8,128)(2,1)}) custom-call(s32[2,64]{1,0:T(2,128)} %pad_add_fusion.2.slots_ref, bf16[64,64,128]{2,1,0:T(8,128)(2,1)} %atm_ref.3, bf16[48,64,128]{2,1,0:T(8,128)(2,1)} %sea_ref.3, f32[2,32,1,256]{3,2,1,0:T(1,128)} %fusion.pos_ref, f32[2,32,1,256]{3,2,1,0:T(1,128)} %get-tuple-element.6.high_ref, ...), custom_call_target="tpu_custom_call" | custom-call | tf_op jit(solution)/shard_map/pack/pallas_call | solution.py:364
  46.8 75.7 %send.1 = bf16[10,17,128,128]{3,2,1,0:T(8,128)(2,1)} custom-call(bf16[9,17,128,128]{3,2,1,0:T(8,128)(2,1)} %get-tuple-element.4.packed_ref), custom_call_target="tpu_custom_call" | custom-call | tf_op jit(solution)/shard_map/send/pallas_call | solution.py:376
  122.5 0.8 slice.4
  123.2 0.6 pad_maximum_fusion.1.across_ref
  123.9 0.7 add_convert_fusion.1.flags_ref
  124.6 1.0 broadcast_in_dim.6.taps_ref
  125.6 46.8 %land.1 = bf16[64,224,128]{2,1,0:T(8,128)(2,1)} custom-call(s32[2]{0:T(128)} %add_convert_fusion.1.flags_ref, bf16[170,128,128]{2,1,0:T(8,128)(2,1)} %bitcast.34, bf16[64,112,128]{2,1,0:T(8,128)(2,1)} %get-tuple-element.5.state_ref, bf16[2,112,128]{2,1,0:T(8,128)(2,1)} %pad_maximum_fusion.1.across_ref, f32[9,112,128]{2,1,0:T(8,128)} %broadcast_in_dim.6.taps_ref), custom_call_target="tpu_custom_call" | custom-call | tf_op jit(solution)/shard_map/land/pallas_call | solution.py:401
  172.4 6.0 %all-to-all-start = ((bf16[2,32,224,128]{3,2,1,0:T(8,128)(2,1)}), bf16[2,32,224,128]{3,2,1,0:T(8,128)(2,1)}, u32[]{:S(2)}, u32[]{:S(2)}) async-start(bf16[2,32,224,128]{3,2,1,0:T(8,128)(2,1)} %bitcast.35), calls=%async_computation | async-start | bytes 7340032 | tf_op jit(solution)/shard_map/all_to_all | solution.py:414
  178.5 0.7 copy.47.coup_a
  179.2 0.7 copy.48.vec_a
  179.9 0.8 copy.49.eb_a
  180.8 0.7 copy.50.vec_o
  181.5 0.8 copy.51.eb_o
  182.2 12.3 %mix.1 = bf16[2,32,112,128]{3,2,1,0:T(8,128)(2,1)} custom-call(bf16[2,32,224,128]{3,2,1,0:T(8,128)(2,1)} %all-to-all-done.in_ref, bf16[128,96]{1,0:T(8,128)(2,1)} %copy.47.coup_a, f32[128,2]{1,0:T(8,128)} %copy.48.vec_a, bf16[256,128]{1,0:T(8,128)(2,1)} %exp_a.1, f32[256,1]{1,0:T(8,128)} %copy.49.eb_a, bf16[128,256]{1,0:T(8,128)(2,1)} %proj_a.1, ...), custom_call_target="tpu_custom_call" | custom-call | tf_op jit(solution)/shard_map/mix/pallas_call | solution.py:425
  194.6 8.2 %all_to_all.10 = bf16[2,32,112,128]{3,2,1,0:T(8,128)(2,1)} all-to-all(bf16[2,32,112,128]{3,2,1,0:T(8,128)(2,1)} %mix.1), channel_id=1, replica_groups=mesh['groups'=2,'tiles'=4,'rows'=2,'comp'=2] {'comp'}, dimensions={0} | all-to-all | bytes 3670016 | tf_op jit(solution)/shard_map/all_to_all | solution.py:434
  202.8 4.4 %finish.1 = (bf16[64,64,128]{2,1,0:T(8,128)(2,1)}, bf16[48,64,128]{2,1,0:T(8,128)(2,1)}) custom-call(bf16[64,112,128]{2,1,0:T(8,128)(2,1)} %bitcast.36, bf16[64,64,128]{2,1,0:T(8,128)(2,1)} %atm_ref.3, bf16[48,64,128]{2,1,0:T(8,128)(2,1)} %sea_ref.3), custom_call_target="tpu_custom_call" | custom-call | tf_op jit(solution)/shard_map/finish/pallas_call | solution.py:440
  (24 shorter events, 0.7 us)
Async XLA Ops:
  46.8 77.1 %copy-start.1 = (f32[48,3,3]{0,2,1:T(4,128)S(1)}, f32[48,3,3]{0,2,1:T(4,128)}, u32[]{:S(2)}) copy-start(f32[48,3,3]{0,2,1:T(4,128)} %param.33) | copy-start | bytes 5188
  46.8 77.1 %copy-start.2 = (f32[64,3,3]{0,2,1:T(4,128)S(1)}, f32[64,3,3]{0,2,1:T(4,128)}, u32[]{:S(2)}) copy-start(f32[64,3,3]{0,2,1:T(4,128)} %param.26) | copy-start | bytes 6916
  172.4 6.1 %copy-start = (bf16[128,96]{0,1:T(8,128)(2,1)S(1)}, bf16[128,96]{0,1:T(8,128)(2,1)}, u32[]{:S(2)}) copy-start(bf16[128,96]{0,1:T(8,128)(2,1)} %param.27) | copy-start | bytes 73732
  172.4 6.8 %copy-start.5 = (f32[128]{0:T(128)S(1)}, f32[128]{0:T(128)}, u32[]{:S(2)}) copy-start(f32[128]{0:T(128)} %param.29) | copy-start | bytes 1540
  172.4 6.8 %copy-start.6 = (f32[128]{0:T(128)S(1)}, f32[128]{0:T(128)}, u32[]{:S(2)}) copy-start(f32[128]{0:T(128)} %param.28) | copy-start | bytes 1540
  172.4 7.6 %copy-start.3 = (f32[256]{0:T(256)S(1)}, f32[256]{0:T(256)}, u32[]{:S(2)}) copy-start(f32[256]{0:T(256)} %param.31) | copy-start | bytes 3076
  172.4 8.3 %copy-start.7 = (f32[96]{0:T(128)S(1)}, f32[96]{0:T(128)}, u32[]{:S(2)}) copy-start(f32[96]{0:T(128)} %param.36) | copy-start | bytes 1156
  172.4 8.3 %copy-start.8 = (f32[96]{0:T(128)S(1)}, f32[96]{0:T(128)}, u32[]{:S(2)}) copy-start(f32[96]{0:T(128)} %param.35) | copy-start | bytes 1156
  172.4 9.1 %copy-start.4 = (f32[192]{0:T(256)S(1)}, f32[192]{0:T(256)}, u32[]{:S(2)}) copy-start(f32[192]{0:T(256)} %param.38) | copy-start | bytes 2308
  172.4 9.8 %all-to-all-start = ((bf16[2,32,224,128]{3,2,1,0:T(8,128)(2,1)}), bf16[2,32,224,128]{3,2,1,0:T(8,128)(2,1)}, u32[]{:S(2)}, u32[]{:S(2)}) async-start(bf16[2,32,224,128]{3,2,1,0:T(8,128)(2,1)} %bitcast.35), calls=%async_computation | async-start | bytes 7340032 | tf_op jit(solution)/shard_map/all_to_all | solution.py:414

commit v3 on v2

--- a/solution.py
+++ b/solution.py
@@ -8,6 +8,7 @@
 from jax.sharding import PartitionSpec as P
 
 SLOTS = 16
+LEVELS = (8, 10, 12, 16)
 META = 112
 LANES = 256
 GROUP = 8
@@ -26,7 +27,7 @@
             state_ref[y : y + 16, low:high, :] = jnp.swapaxes(field[:, y : y + 16, :], 0, 1)
 
     def clear(i, _):
-        out_ref[i // SLOTS, lax.rem(i, SLOTS), META:, :] = jnp.full((16, 128), -1, BF)
+        out_ref[i // SLOTS, lax.rem(i, SLOTS) + 1, META:, :] = jnp.full((16, 128), -1, BF)
         return 0
 
     lax.fori_loop(0, 9 * SLOTS, clear, 0)
@@ -41,13 +42,13 @@
     columns = lax.fori_loop(0, height, column_of, jnp.zeros((chans_all, LANES), F32)).astype(BF)
     for k in range(9):
         if k // 3 == 0:
-            out_ref[k, SLOTS, :chans_all, :] = state_ref[0]
+            out_ref[k, 0, :chans_all, :] = state_ref[0]
         elif k // 3 == 2:
-            out_ref[k, SLOTS, :chans_all, :] = state_ref[height - 1]
+            out_ref[k, 0, :chans_all, :] = state_ref[height - 1]
         elif k == 3:
-            out_ref[k, SLOTS, :chans_all, :] = columns[:, :128]
+            out_ref[k, 0, :chans_all, :] = columns[:, :128]
         elif k == 5:
-            out_ref[k, SLOTS, :chans_all, :] = columns[:, 128:]
+            out_ref[k, 0, :chans_all, :] = columns[:, 128:]
 
     column = lax.broadcasted_iota(jnp.int32, (LANES, LANES), 0).astype(F32).astype(BF)
     row16 = lax.broadcasted_iota(jnp.int32, (16, 128), 0)
@@ -57,8 +58,8 @@
             chans = high - low
             hit = jnp.broadcast_to(pos_ref[f, j], (LANES, LANES)).astype(BF) == column
             onehot = jnp.where(hit, jnp.ones((), BF), jnp.zeros((), BF))
-            wanted = jnp.broadcast_to(high_ref[f, j], (chans, LANES))
-            total = jnp.zeros((chans, LANES), F32)
+            wanted = jnp.broadcast_to(high_ref[f, j], (8, LANES))
+            total = jnp.zeros((chans // 8, 8, LANES), F32)
             for first in range(0, pairs, GROUP):
                 lhs = jnp.concatenate(
                     [
@@ -71,14 +72,13 @@
                 )
                 part = jnp.dot(lhs, onehot, preferred_element_type=F32)
                 for q in range(GROUP):
-                    total = jnp.where(
-                        wanted == float(first + q), part[q * chans : (q + 1) * chans], total
-                    )
-            values = (total * weight_ref[f, j]).astype(BF)
+                    piece = part[q * chans : (q + 1) * chans].reshape(total.shape)
+                    total = jnp.where((wanted == float(first + q))[None], piece, total)
+            values = (total.reshape(chans, LANES) * weight_ref[f, j]).astype(BF)
             for half in range(2):
                 block = 2 * j + half
                 slot = slots_ref[f, block]
-                k, s = slot // SLOTS, lax.rem(slot, SLOTS)
+                k, s = slot // SLOTS, lax.rem(slot, SLOTS) + 1
                 out_ref[k, s, low:high, :] = values[:, half * 128 : (half + 1) * 128]
                 old = out_ref[k, s, META:, :].astype(F32)
                 for item in range(2):
@@ -90,7 +90,7 @@
     lax.fori_loop(0, slots_ref.shape[1] // 2, step, 0)
 
 
-def send_kernel(n_tiles, n_rows, packed_ref, got_ref, send_sem, recv_sem, local_sem):
+def send_kernel(n_tiles, n_rows, cap, packed_ref, got_ref, send_sem, recv_sem, local_sem):
     band = lax.axis_index("tiles")
     strip = lax.axis_index("rows")
     last = n_tiles - 1
@@ -125,8 +125,8 @@
     def copy(i):
         src, dst, to, _, _ = routes[i]
         return pltpu.make_async_remote_copy(
-            src_ref=packed_ref.at[src],
-            dst_ref=got_ref.at[dst],
+            src_ref=packed_ref.at[src, pl.ds(0, cap + 1)],
+            dst_ref=got_ref.at[dst, pl.ds(0, cap + 1)],
             send_sem=send_sem.at[i],
             recv_sem=recv_sem.at[i],
             device_id=to,
@@ -164,7 +164,7 @@
     is_air = lax.broadcasted_iota(jnp.int32, (chans, 128), 0) < bounds[0][1]
 
     def edge(k):
-        return got_ref[k * stride + SLOTS, :chans, :]
+        return got_ref[k * stride, :chans, :]
 
     cols = jnp.concatenate([edge(5), edge(3)], axis=1)
     wide = lax.broadcasted_iota(jnp.int32, (chans, 256), 1) % 128
@@ -230,10 +230,11 @@
     pairs = height // 2
     place_row = lax.broadcasted_iota(jnp.int32, (16, 128), 0)
     place_lane = lax.broadcasted_iota(jnp.int32, (16, 128), 1)
+    slot_at = lax.broadcasted_iota(jnp.int32, (SLOTS, 16, 128), 0)
     counts = [jnp.int32(0), jnp.int32(0)]
     for k in range(10):
-        places = got_ref[k * stride : k * stride + SLOTS, META:, :].astype(F32)
-        filled = jnp.sum((places >= 0).astype(F32), axis=0)
+        places = got_ref[k * stride + 1 : (k + 1) * stride, META:, :].astype(F32)
+        filled = jnp.sum(((places >= 0) & (slot_at < (SLOTS if k == 4 else flags_ref[2]))).astype(F32), axis=0)
         usable = True if 3 <= k < 6 else jnp.logical_not(last_band) if k < 3 else jnp.logical_not(first_band) if k < 9 else last_band
         for f in range(2):
             there = (place_row == 2 * f) & (place_lane == 0)
@@ -242,7 +243,7 @@
             base = counts[f]
 
             def note(i, _):
-                order_ref[f, base + i] = k * stride + i
+                order_ref[f, base + i] = k * stride + 1 + i
                 return 0
 
             lax.fori_loop(0, count, note, 0)
@@ -332,7 +333,8 @@
     n = lanes.shape[0]
     i = jnp.arange(n, dtype=jnp.int32)
     before = (lanes[:, None] == lanes[None, :]) & (i[None, :] < i[:, None])
-    return lanes * SLOTS + jnp.sum(before.astype(jnp.int32), axis=1)
+    within = jnp.sum(before.astype(jnp.int32), axis=1)
+    return lanes * SLOTS + within, jnp.max(jnp.where(lanes == 4, 0, within + 1))
 
 
 def local(
@@ -352,7 +354,11 @@
     vmem = pl.BlockSpec(memory_space=pltpu.VMEM)
     smem = pl.BlockSpec(memory_space=pltpu.SMEM)
 
-    slots = jnp.stack([slots_of(flux_heading), slots_of(sst_heading)])
+    flux_slots, flux_most = slots_of(flux_heading)
+    sst_slots, sst_most = slots_of(sst_heading)
+    slots = jnp.stack([flux_slots, sst_slots])
+    most = lax.pmax(jnp.maximum(flux_most, sst_most), ("groups", "tiles", "rows", "comp"))
+    level = sum((most > cap).astype(jnp.int32) for cap in LEVELS[:-1])
     source = jnp.stack([flux_source, sst_source])
     target = jnp.stack([flux_target, sst_target])
     weight = jnp.stack([flux_weight, sst_weight])
@@ -373,19 +379,22 @@
         name="pack",
     )(slots, atm, sea, paired(source % LANES), paired(source // LANES), paired(weight), meta)
 
-    got = pl.pallas_call(
-        functools.partial(send_kernel, n_tiles, n_rows),
-        out_shape=jax.ShapeDtypeStruct((10, SLOTS + 1, 128, 128), BF),
-        in_specs=[pl.BlockSpec(memory_space=pl.ANY)],
-        out_specs=pl.BlockSpec(memory_space=pl.ANY),
-        scratch_shapes=[
-            pltpu.SemaphoreType.DMA((9,)),
-            pltpu.SemaphoreType.DMA((9,)),
-            pltpu.SemaphoreType.DMA,
-        ],
-        compiler_params=params(collective_id=0, has_side_effects=True),
-        name="send",
-    )(packed)
+    def send(index, cap):
+        return pl.pallas_call(
+            functools.partial(send_kernel, n_tiles, n_rows, cap),
+            out_shape=jax.ShapeDtypeStruct((10, SLOTS + 1, 128, 128), BF),
+            in_specs=[pl.BlockSpec(memory_space=pl.ANY)],
+            out_specs=pl.BlockSpec(memory_space=pl.ANY),
+            scratch_shapes=[
+                pltpu.SemaphoreType.DMA((9,)),
+                pltpu.SemaphoreType.DMA((9,)),
+                pltpu.SemaphoreType.DMA,
+            ],
+            compiler_params=params(collective_id=index, has_side_effects=True),
+            name=f"send{cap}",
+        )
+
+    got = lax.switch(level, [send(index, cap) for index, cap in enumerate(LEVELS)], packed)
 
     def across(side):
         perm = [(s, n_rows - 1 - (s + side) % n_rows) for s in range(n_rows)]
@@ -397,7 +406,8 @@
     taps = jnp.concatenate([atm_kernel, sea_kernel], axis=0).reshape(part, 9).T[:, :, None]
     taps = jnp.broadcast_to(taps, (9, part, 128))
 
-    flags = jnp.stack([band == 0, band == last]).astype(jnp.int32)
+    cap = sum(jnp.where(level == index, cap, 0) for index, cap in enumerate(LEVELS))
+    flags = jnp.stack([(band == 0).astype(jnp.int32), (band == last).astype(jnp.int32), cap])
     mixed_in = pl.pallas_call(
         functools.partial(land_kernel, bounds, (part + half_o, part)),
         out_shape=jax.ShapeDtypeStruct((height, 2 * part, 128), BF),

time: 208 us -> 228 us (1.096)
  blocking collectives: 8.2 us -> 48.1 us
  Pallas kernels: 177 us -> 151 us
  between operations: 0.72 us -> 3.97 us
    pmax x0 -> x1, blocking collectives: none -> 39.9 us  [local(): lax.pmax(jnp.maximum(flux_most, sst_most), ('groups', 'tiles', 'rows', 'c...]
    pallas_call x1, Pallas kernels: 75.7 us -> 50.3 us  [local(): lax.switch(level, [send(index, cap) for index, cap in enumerate(LEVELS)],...]
where the time goes in v3:
time: 228 us; the launch traced here: 227 us
  Pallas kernels  151 us (66%)
  blocking collectives  48.1 us (21%)
  other arithmetic  11.9 us (5%)
  starting transfers between devices  6.11 us (3%)
  local copies, waits for them, and re-layouts  5.52 us (2%)
  between operations  3.97 us (2%)
    pallas_call x1, Pallas kernels, local(): lax.switch(level, [send(index, cap) for index, cap in enumerate(LEVELS)],...  50.3 us
    pallas_call x1, Pallas kernels, local(): pl.pallas_call(functools.partial(land_kernel, bounds, (part + half_o, par...  46.8 us
    pmax x1, blocking collectives, local(): lax.pmax(jnp.maximum(flux_most, sst_most), ('groups', 'tiles', 'rows', 'c...  39.9 us
    pallas_call x1, Pallas kernels, local(): pl.pallas_call(functools.partial(pack_kernel, bounds), out_shape=[jax.Sha...  37.5 us
    pallas_call x1, Pallas kernels, local(): pl.pallas_call(functools.partial(mix_kernel, ca, co), grid=(height // 2 /...  12.3 us
    all_to_all x1, blocking collectives, local(): lax.all_to_all(update, 'comp', split_axis=0, concat_axis=0)  8.21 us
    all_to_all x1, starting transfers between devices, local(): lax.all_to_all(mixed_in.reshape(2, height // 2, 2 * part, 128), 'comp', s...  6.11 us
  transfers between devices with their start and end apart: 1, of which 0 were waited for; matrix products, arithmetic and copies ran while one was open for 2% of the time, Pallas kernels for 0%

profile of v3, /device:TPU:9, one launch (start us, length us, event | category | flops | bytes accessed | tf_op | source)
XLA Modules:
  0.0 226.9 jit_solution(11969596951953571130)
XLA Ops:
  0.6 0.9 convert_reduce_fusion
  1.5 0.9 convert_reduce_fusion.1
  2.5 1.3 fusion.5
  5.1 39.9 %pmax.7 = s32[]{:T(128)} all-reduce(s32[]{:T(128)S(6)} %max.5), channel_id=1, replica_groups=mesh['groups'=2,'tiles'=4,'rows'=2,'comp'=2] {'groups','tiles','rows','c..., use_global_device_ids=true, to_apply=%region_4.5 | all-reduce | flops 1 | bytes 8 | tf_op jit(solution)/shard_map/pmax | solution.py:360
  47.6 1.7 fusion.2
  49.3 0.7 fusion.pos_ref
  50.6 0.8 add_select_fusion.1
  51.5 0.7 add_convert_fusion.meta_ref
  52.2 1.5 pad_maximum_fusion.weight_ref
  53.7 37.5 %pack.1 = (bf16[9,17,128,128]{3,2,1,0:T(8,128)(2,1)}, bf16[64,112,128]{2,1,0:T(8,128)(2,1)}) custom-call(s32[2,64]{1,0:T(2,128)} %pad_add_fusion.2.slots_ref, bf16[64,64,128]{2,1,0:T(8,128)(2,1)} %atm_ref.3, bf16[48,64,128]{2,1,0:T(8,128)(2,1)} %sea_ref.3, f32[2,32,1,256]{3,2,1,0:T(1,128)} %fusion.pos_ref, f32[2,32,1,256]{3,2,1,0:T(1,128)} %get-tuple-element.16.high_ref, ...), custom_call_target="tpu_custom_call" | custom-call | tf_op jit(solution)/shard_map/pack/pallas_call | solution.py:370
  91.2 0.8 slice.4
  92.6 0.8 pad_maximum_fusion.2
  93.4 50.3 %conditional.1 = (bf16[170,128,128]{2,1,0:T(8,128)(2,1)}) conditional(s32[]{:T(128)} %clamp.3, bf16[9,17,128,128]{3,2,1,0:T(8,128)(2,1)} %get-tuple-element.14, bf16[9,17,128,128]{3,2,1,0:T(8,128)(2,1)} %get-tuple-element.14, bf16[9,17,128,128]{3,2,1,0:T(8,128)(2,1)} %get-tuple-element.14, ...), branch_computations={%region_5.6_spmd, %region_6.7_spmd, %region_7.8_spmd, %region_8.9_... | conditional | bytes 8 | solution.py:397
  93.4 50.3 %send10.1 = bf16[10,17,128,128]{3,2,1,0:T(8,128)(2,1)} custom-call(bf16[9,17,128,128]{3,2,1,0:T(8,128)(2,1)} %packed_ref.1), custom_call_target="tpu_custom_call" | custom-call | tf_op jit(solution)/shard_map/cond/branch_1_fun/send10/pallas_call | solution.py:397
  144.3 1.0 broadcast_in_dim.12.taps_ref
  145.2 46.8 %land.1 = bf16[64,224,128]{2,1,0:T(8,128)(2,1)} custom-call(s32[3]{0:T(128)} %pad_add_fusion.3.flags_ref, bf16[170,128,128]{2,1,0:T(8,128)(2,1)} %get-tuple-element.24.got_ref, bf16[64,112,128]{2,1,0:T(8,128)(2,1)} %get-tuple-element.15.state_ref, bf16[2,112,128]{2,1,0:T(8,128)(2,1)} %pad_maximum_fusion.1.across_ref, f32[9,112,128]{2,1,0:T(8,128)} %broadcast_in_dim.12.taps_ref), custom_call_target="tpu_custom_call" | custom-call | tf_op jit(solution)/shard_map/land/pallas_call | solution.py:411
  192.1 6.1 %all-to-all-start = ((bf16[2,32,224,128]{3,2,1,0:T(8,128)(2,1)}), bf16[2,32,224,128]{3,2,1,0:T(8,128)(2,1)}, u32[]{:S(2)}, u32[]{:S(2)}) async-start(bf16[2,32,224,128]{3,2,1,0:T(8,128)(2,1)} %bitcast.44), calls=%async_computation | async-start | bytes 7340032 | tf_op jit(solution)/shard_map/all_to_all | solution.py:424
  198.2 0.8 copy.49.eb_a
  199.0 0.8 copy.51.eb_o
  199.8 0.7 copy.48.vec_a
  200.5 0.7 copy.50.vec_o
  202.0 12.3 %mix.1 = bf16[2,32,112,128]{3,2,1,0:T(8,128)(2,1)} custom-call(bf16[2,32,224,128]{3,2,1,0:T(8,128)(2,1)} %all-to-all-done.in_ref, bf16[128,96]{1,0:T(8,128)(2,1)} %copy.47.coup_a, f32[128,2]{1,0:T(8,128)} %copy.48.vec_a, bf16[256,128]{1,0:T(8,128)(2,1)} %exp_a.1, f32[256,1]{1,0:T(8,128)} %copy.49.eb_a, bf16[128,256]{1,0:T(8,128)(2,1)} %proj_a.1, ...), custom_call_target="tpu_custom_call" | custom-call | tf_op jit(solution)/shard_map/mix/pallas_call | solution.py:435
  214.3 8.2 %all_to_all.10 = bf16[2,32,112,128]{3,2,1,0:T(8,128)(2,1)} all-to-all(bf16[2,32,112,128]{3,2,1,0:T(8,128)(2,1)} %mix.1), channel_id=1, replica_groups=mesh['groups'=2,'tiles'=4,'rows'=2,'comp'=2] {'comp'}, dimensions={0} | all-to-all | bytes 3670016 | tf_op jit(solution)/shard_map/all_to_all | solution.py:444
  222.5 4.4 %finish.1 = (bf16[64,64,128]{2,1,0:T(8,128)(2,1)}, bf16[48,64,128]{2,1,0:T(8,128)(2,1)}) custom-call(bf16[64,112,128]{2,1,0:T(8,128)(2,1)} %bitcast.45, bf16[64,64,128]{2,1,0:T(8,128)(2,1)} %atm_ref.3, bf16[48,64,128]{2,1,0:T(8,128)(2,1)} %sea_ref.3), custom_call_target="tpu_custom_call" | custom-call | tf_op jit(solution)/shard_map/finish/pallas_call | solution.py:450
  (23 shorter events, 3.3 us)
Async XLA Ops:
  192.0 6.2 %copy-start.1 = (f32[256]{0:T(256)S(1)}, f32[256]{0:T(256)}, u32[]{:S(2)}) copy-start(f32[256]{0:T(256)} %param.35) | copy-start | bytes 3076
  192.0 7.0 %copy-start.2 = (f32[192]{0:T(256)S(1)}, f32[192]{0:T(256)}, u32[]{:S(2)}) copy-start(f32[192]{0:T(256)} %param.42) | copy-start | bytes 2308
  192.0 7.7 %copy-start.3 = (f32[128]{0:T(128)S(1)}, f32[128]{0:T(128)}, u32[]{:S(2)}) copy-start(f32[128]{0:T(128)} %param.33) | copy-start | bytes 1540
  192.0 7.7 %copy-start.4 = (f32[128]{0:T(128)S(1)}, f32[128]{0:T(128)}, u32[]{:S(2)}) copy-start(f32[128]{0:T(128)} %param.32) | copy-start | bytes 1540
  192.0 8.5 %copy-start.5 = (f32[96]{0:T(128)S(1)}, f32[96]{0:T(128)}, u32[]{:S(2)}) copy-start(f32[96]{0:T(128)} %param.40) | copy-start | bytes 1156
  192.1 8.5 %copy-start.6 = (f32[96]{0:T(128)S(1)}, f32[96]{0:T(128)}, u32[]{:S(2)}) copy-start(f32[96]{0:T(128)} %param.39) | copy-start | bytes 1156
  192.1 9.2 %copy-start = (bf16[128,96]{0,1:T(8,128)(2,1)S(1)}, bf16[128,96]{0,1:T(8,128)(2,1)}, u32[]{:S(2)}) copy-start(bf16[128,96]{0,1:T(8,128)(2,1)} %param.31) | copy-start | bytes 73732
  192.1 9.9 %all-to-all-start = ((bf16[2,32,224,128]{3,2,1,0:T(8,128)(2,1)}), bf16[2,32,224,128]{3,2,1,0:T(8,128)(2,1)}, u32[]{:S(2)}, u32[]{:S(2)}) async-start(bf16[2,32,224,128]{3,2,1,0:T(8,128)(2,1)} %bitcast.44), calls=%async_computation | async-start | bytes 7340032 | tf_op jit(solution)/shard_map/all_to_all | solution.py:424

commit v4 on v3

--- a/solution.py
+++ b/solution.py
@@ -357,7 +357,14 @@
     flux_slots, flux_most = slots_of(flux_heading)
     sst_slots, sst_most = slots_of(sst_heading)
     slots = jnp.stack([flux_slots, sst_slots])
-    most = lax.pmax(jnp.maximum(flux_most, sst_most), ("groups", "tiles", "rows", "comp"))
+    most = jnp.broadcast_to(jnp.maximum(flux_most, sst_most), (1, 128)).astype(jnp.int32)
+    for axis, count in (("rows", n_rows), ("tiles", n_tiles)):
+        shift = 1
+        while shift < count:
+            ring = [(i, (i + shift) % count) for i in range(count)]
+            most = jnp.maximum(most, lax.ppermute(most, axis, ring))
+            shift *= 2
+    most = most[0, 0]
     level = sum((most > cap).astype(jnp.int32) for cap in LEVELS[:-1])
     source = jnp.stack([flux_source, sst_source])
     target = jnp.stack([flux_target, sst_target])
@@ -376,6 +383,7 @@
         in_specs=[smem] + [vmem] * 6,
         out_specs=[vmem, vmem],
         compiler_params=params(),
+        cost_estimate=pl.CostEstimate(flops=20_000_000_000, bytes_accessed=10_000_000, transcendentals=0),
         name="pack",
     )(slots, atm, sea, paired(source % LANES), paired(source // LANES), paired(weight), meta)
 

time: 228 us -> 197 us (0.86)
  blocking collectives: 48.1 us -> 20 us
    pmax x1 -> x0, blocking collectives: 39.9 us -> none  [local(): lax.pmax(jnp.maximum(flux_most, sst_most), ('groups', 'tiles', 'rows', 'c...]
    all_to_all x0 -> x1, blocking collectives: none -> 11.7 us  [local(): lax.all_to_all(mixed_in.reshape(2, height // 2, 2 * part, 128), 'comp', s...]
    all_to_all x1 -> x0, starting transfers between devices: 6.11 us -> none  [local(): lax.all_to_all(mixed_in.reshape(2, height // 2, 2 * part, 128), 'comp', s...]
    ppermute x0 -> x3, starting transfers between devices: none -> 4.93 us  [local(): most = jnp.maximum(most, lax.ppermute(most, axis, ring))]
  transfers between devices with their start and end apart: 1 -> 3, of which waited for: 0 -> 1; matrix products, arithmetic and copies ran while one was open for 2% -> 6% of each run, Pallas kernels for 0% -> 19%
where the time goes in v4:
time: 197 us; the launch traced here: 196 us
  Pallas kernels  151 us (77%)
  blocking collectives  20 us (10%)
  other arithmetic  11.3 us (6%)
  local copies, waits for them, and re-layouts  5.51 us (3%)
  starting transfers between devices  4.93 us (3%)
  between operations  2.22 us (1%)
    pallas_call x1, Pallas kernels, local(): lax.switch(level, [send(index, cap) for index, cap in enumerate(LEVELS)],...  49.8 us
    pallas_call x1, Pallas kernels, local(): pl.pallas_call(functools.partial(land_kernel, bounds, (part + half_o, par...  46.7 us
    pallas_call x1, Pallas kernels, local(): pl.pallas_call(functools.partial(pack_kernel, bounds), out_shape=[jax.Sha...  37.6 us
    pallas_call x1, Pallas kernels, local(): pl.pallas_call(functools.partial(mix_kernel, ca, co), grid=(height // 2 /...  12.3 us
    all_to_all x1, blocking collectives, local(): lax.all_to_all(mixed_in.reshape(2, height // 2, 2 * part, 128), 'comp', s...  11.7 us
    all_to_all x1, blocking collectives, local(): lax.all_to_all(update, 'comp', split_axis=0, concat_axis=0)  8.29 us
    ppermute x3, starting transfers between devices, local(): most = jnp.maximum(most, lax.ppermute(most, axis, ring))  4.93 us
    pallas_call x1, Pallas kernels, local(): pl.pallas_call(functools.partial(finish_kernel, bounds), grid=(height //...  4.38 us
  transfers between devices with their start and end apart: 3, of which 1 were waited for; matrix products, arithmetic and copies ran while one was open for 6% of the time, Pallas kernels for 19%

profile of v4, /device:TPU:9, one launch (start us, length us, event | category | flops | bytes accessed | tf_op | source)
XLA Modules:
  0.0 195.9 jit_solution(16329445471711058745)
XLA Ops:
  0.6 0.9 convert_reduce_fusion
  1.5 0.9 convert_reduce_fusion.1
  2.5 1.3 fusion.5
  5.1 1.3 collective-permute-start
  7.0 1.7 fusion.2
  10.0 0.8 add_select_fusion.1
  10.9 0.7 add_convert_fusion.meta_ref
  11.6 1.5 pad_maximum_fusion.weight_ref
  13.2 37.6 %pack.1 = (bf16[9,17,128,128]{3,2,1,0:T(8,128)(2,1)}, bf16[64,112,128]{2,1,0:T(8,128)(2,1)}) custom-call(s32[2,64]{1,0:T(2,128)} %pad_add_fusion.2.slots_ref, bf16[64,64,128]{2,1,0:T(8,128)(2,1)} %atm_ref.3, bf16[48,64,128]{2,1,0:T(8,128)(2,1)} %sea_ref.3, f32[2,32,1,256]{3,2,1,0:T(1,128)} %fusion.pos_ref, f32[2,32,1,256]{3,2,1,0:T(1,128)} %get-tuple-element.16.high_ref, ...), custom_call_target="tpu_custom_call" | custom-call | flops 20000000000 | bytes 10000000 | tf_op jit(solution)/shard_map/pack/pallas_call | solution.py:377
  50.8 0.8 slice.8
  52.3 1.3 collective-permute-start.1
  53.7 1.1 collective-permute-done.1
  54.8 2.3 %collective-permute-start.2 = (s32[1,128]{1,0:T(1,128)S(1)}, s32[1,128]{1,0:T(1,128)S(1)}, u32[]{:S(2)}, u32[]{:S(2)}) collective-permute-start(s32[1,128]{1,0:T(1,128)S(1)} %fusion.7), channel_id=1, source_target_pairs={{0,8},{4,12},{8,0},{12,4},{1,9},{5,13},{9,1},{13,5},{2,10},{6,14},... | collective-permute-start | bytes 1544 | tf_op jit(solution)/shard_map/ppermute | solution.py:365
  57.1 0.8 copy.49.eb_a
  57.9 0.8 copy.51.eb_o
  58.6 0.7 copy.48.vec_a
  60.9 49.8 %conditional.1 = (bf16[170,128,128]{2,1,0:T(8,128)(2,1)}) conditional(s32[]{:T(128)} %bitcast.9, bf16[9,17,128,128]{3,2,1,0:T(8,128)(2,1)} %get-tuple-element.14, bf16[9,17,128,128]{3,2,1,0:T(8,128)(2,1)} %get-tuple-element.14, bf16[9,17,128,128]{3,2,1,0:T(8,128)(2,1)} %get-tuple-element.14, ...), branch_computations={%region_4.5_spmd, %region_5.6_spmd, %region_6.7_spmd, %region_7.8_... | conditional | bytes 8 | solution.py:405
  61.0 49.8 %send10.1 = bf16[10,17,128,128]{3,2,1,0:T(8,128)(2,1)} custom-call(bf16[9,17,128,128]{3,2,1,0:T(8,128)(2,1)} %packed_ref.1), custom_call_target="tpu_custom_call" | custom-call | tf_op jit(solution)/shard_map/cond/branch_1_fun/send10/pallas_call | solution.py:405
  111.4 1.0 broadcast_in_dim.27.taps_ref
  112.4 46.7 %land.1 = bf16[64,224,128]{2,1,0:T(8,128)(2,1)} custom-call(s32[3]{0:T(128)} %pad_add_fusion.3.flags_ref, bf16[170,128,128]{2,1,0:T(8,128)(2,1)} %get-tuple-element.24.got_ref, bf16[64,112,128]{2,1,0:T(8,128)(2,1)} %get-tuple-element.15.state_ref, bf16[2,112,128]{2,1,0:T(8,128)(2,1)} %pad_maximum_fusion.1.across_ref, f32[9,112,128]{2,1,0:T(8,128)} %broadcast_in_dim.27.taps_ref), custom_call_target="tpu_custom_call" | custom-call | tf_op jit(solution)/shard_map/land/pallas_call | solution.py:419
  159.2 11.7 %all_to_all.10.in_ref = bf16[2,32,224,128]{3,2,1,0:T(8,128)(2,1)} all-to-all(bf16[2,32,224,128]{3,2,1,0:T(8,128)(2,1)} %bitcast.46), channel_id=1, replica_groups=mesh['groups'=2,'tiles'=4,'rows'=2,'comp'=2] {'comp'}, dimensions={0} | all-to-all | bytes 7340032 | tf_op jit(solution)/shard_map/all_to_all | solution.py:432
  170.9 12.3 %mix.1 = bf16[2,32,112,128]{3,2,1,0:T(8,128)(2,1)} custom-call(bf16[2,32,224,128]{3,2,1,0:T(8,128)(2,1)} %all_to_all.10.in_ref, bf16[128,96]{1,0:T(8,128)(2,1)} %copy.47.coup_a, f32[128,2]{1,0:T(8,128)} %copy.48.vec_a, bf16[256,128]{1,0:T(8,128)(2,1)} %exp_a.1, f32[256,1]{1,0:T(8,128)} %copy.49.eb_a, bf16[128,256]{1,0:T(8,128)(2,1)} %proj_a.1, ...), custom_call_target="tpu_custom_call" | custom-call | tf_op jit(solution)/shard_map/mix/pallas_call | solution.py:443
  183.2 8.3 %all_to_all.11 = bf16[2,32,112,128]{3,2,1,0:T(8,128)(2,1)} all-to-all(bf16[2,32,112,128]{3,2,1,0:T(8,128)(2,1)} %mix.1), channel_id=1, replica_groups=mesh['groups'=2,'tiles'=4,'rows'=2,'comp'=2] {'comp'}, dimensions={0} | all-to-all | bytes 3670016 | tf_op jit(solution)/shard_map/all_to_all | solution.py:452
  191.5 4.4 %finish.1 = (bf16[64,64,128]{2,1,0:T(8,128)(2,1)}, bf16[48,64,128]{2,1,0:T(8,128)(2,1)}) custom-call(bf16[64,112,128]{2,1,0:T(8,128)(2,1)} %bitcast.47, bf16[64,64,128]{2,1,0:T(8,128)(2,1)} %atm_ref.3, bf16[48,64,128]{2,1,0:T(8,128)(2,1)} %sea_ref.3), custom_call_target="tpu_custom_call" | custom-call | tf_op jit(solution)/shard_map/finish/pallas_call | solution.py:458
  (35 shorter events, 4.9 us)
Async XLA Ops:
  5.1 47.2 %collective-permute-start = (s32[1,128]{1,0:T(1,128)S(1)}, s32[1,128]{1,0:T(1,128)S(1)}, u32[]{:S(2)}, u32[]{:S(2)}) collective-permute-start(s32[1,128]{1,0:T(1,128)S(1)} %broadcast_in_dim.26), channel_id=1, source_target_pairs={{0,2},{2,0},{1,3},{3,1},{4,6},{6,4},{5,7},{7,5},{8,10},{10,8},{9,1... | collective-permute-start | bytes 1544 | tf_op jit(solution)/shard_map/ppermute | solution.py:365
  13.1 39.1 %copy-start.1 = (f32[48,3,3]{0,2,1:T(4,128)S(1)}, f32[48,3,3]{0,2,1:T(4,128)}, u32[]{:S(2)}) copy-start(f32[48,3,3]{0,2,1:T(4,128)} %param.37) | copy-start | bytes 5188
  13.1 39.1 %copy-start.2 = (f32[64,3,3]{0,2,1:T(4,128)S(1)}, f32[64,3,3]{0,2,1:T(4,128)}, u32[]{:S(2)}) copy-start(f32[64,3,3]{0,2,1:T(4,128)} %param.30) | copy-start | bytes 6916
  13.1 39.1 %copy-start.5 = (f32[128]{0:T(128)S(1)}, f32[128]{0:T(128)}, u32[]{:S(2)}) copy-start(f32[128]{0:T(128)} %param.33) | copy-start | bytes 1540
  13.1 39.1 %copy-start.6 = (f32[128]{0:T(128)S(1)}, f32[128]{0:T(128)}, u32[]{:S(2)}) copy-start(f32[128]{0:T(128)} %param.32) | copy-start | bytes 1540
  13.1 39.2 %copy-start.7 = (f32[96]{0:T(128)S(1)}, f32[96]{0:T(128)}, u32[]{:S(2)}) copy-start(f32[96]{0:T(128)} %param.40) | copy-start | bytes 1156
  13.1 39.2 %copy-start.8 = (f32[96]{0:T(128)S(1)}, f32[96]{0:T(128)}, u32[]{:S(2)}) copy-start(f32[96]{0:T(128)} %param.39) | copy-start | bytes 1156
  13.1 43.9 %copy-start.3 = (f32[256]{0:T(256)S(1)}, f32[256]{0:T(256)}, u32[]{:S(2)}) copy-start(f32[256]{0:T(256)} %param.35) | copy-start | bytes 3076
  13.1 44.7 %copy-start.4 = (f32[192]{0:T(256)S(1)}, f32[192]{0:T(256)}, u32[]{:S(2)}) copy-start(f32[192]{0:T(256)} %param.42) | copy-start | bytes 2308
  13.1 46.9 %copy-start = (bf16[128,96]{0,1:T(8,128)(2,1)S(1)}, bf16[128,96]{0,1:T(8,128)(2,1)}, u32[]{:S(2)}) copy-start(bf16[128,96]{0,1:T(8,128)(2,1)} %param.31) | copy-start | bytes 73732
  52.3 2.4 %collective-permute-start.1 = (s32[1,128]{1,0:T(1,128)S(1)}, s32[1,128]{1,0:T(1,128)S(1)}, u32[]{:S(2)}, u32[]{:S(2)}) collective-permute-start(s32[1,128]{1,0:T(1,128)S(1)} %broadcast_maximum_fusion), channel_id=1, source_target_pairs={{0,4},{4,8},{8,12},{12,0},{1,5},{5,9},{9,13},{13,1},{2,6},{6,10},{... | collective-permute-start | bytes 1544 | tf_op jit(solution)/shard_map/ppermute | solution.py:365
  54.8 6.0 %collective-permute-start.2 = (s32[1,128]{1,0:T(1,128)S(1)}, s32[1,128]{1,0:T(1,128)S(1)}, u32[]{:S(2)}, u32[]{:S(2)}) collective-permute-start(s32[1,128]{1,0:T(1,128)S(1)} %fusion.7), channel_id=1, source_target_pairs={{0,8},{4,12},{8,0},{12,4},{1,9},{5,13},{9,1},{13,5},{2,10},{6,14},... | collective-permute-start | bytes 1544 | tf_op jit(solution)/shard_map/ppermute | solution.py:365
